TPU v7x, 32 devices: a whole 2x2x4 slice. The times are simulated.
32 devices in a mesh: dp: 8 (over y, x, core), tensor: 4 (over z).
Axes of the slice: x: 2, y: 2, z: 4, core: 2. Of those that a mesh axis runs over, the one named last changes fastest.
Arguments:
- hidden_in: bfloat16 [8, 1024, 2048], P('dp', 'tensor'), may hold values from -6 to 6
- out_grad: bfloat16 [8, 1024, 2048], P('dp', 'tensor'), may hold values from -6 to 6
- doc_ids: int32 [8, 1024], P('dp'), may hold values from 0 to 1023, as said below
- expert_ids: int32 [8, 1024, 8], P('dp'), may hold values from 0 to 63, all different within a row; in each aligned block of 1024 rows (0 to 1023, 1024 to 2047, ..., all dimensions but the last counted through in order) at most 192 rows name the same one
- prenorm: bfloat16 [2048], P(('dp', 'tensor')), may hold values from 0.099609375 to 1.8984375
- querynorm: bfloat16 [128, 16], P('dp', 'tensor'), may hold values from 0.099609375 to 1.8984375
- keynorm: bfloat16 [128, 16], P('dp', 'tensor'), may hold values from 0.099609375 to 1.8984375
- query_proj: bfloat16 [2048, 2048], P('dp', 'tensor'), may hold values from -0.125 to 0.125
- key_proj: bfloat16 [2048, 2048], P('dp', 'tensor'), may hold values from -0.125 to 0.125
- value_proj: bfloat16 [2048, 2048], P('dp', 'tensor'), may hold values from -0.125 to 0.125
- output_proj: bfloat16 [2048, 2048], P('dp', 'tensor'), may hold values from -1.5 to 1.5
- postnorm: bfloat16 [2048], P(('dp', 'tensor')), may hold values from 0.099609375 to 1.8984375
- router: bfloat16 [2048, 64], P(('dp', 'tensor')), may hold values from -0.0625 to 0.0625
- gate_proj: bfloat16 [64, 2048, 1024], P('dp', None, 'tensor'), may hold values from -0.125 to 0.125
- up_proj: bfloat16 [64, 2048, 1024], P('dp', None, 'tensor'), may hold values from -0.125 to 0.125
- down_proj: bfloat16 [64, 2048, 1024], P('dp', None, 'tensor'), may hold values from -6 to 6
Outputs:
- layer_out: bfloat16 [8, 1024, 2048], P('dp', 'tensor')
- input_grad: bfloat16 [8, 1024, 2048], P('dp', 'tensor')
- prenorm_grad: float32 [2048], P(('dp', 'tensor'))
- querynorm_grad: float32 [128, 16], P('dp', 'tensor')
- keynorm_grad: float32 [128, 16], P('dp', 'tensor')
- query_grad: float32 [2048, 2048], P('dp', 'tensor')
- key_grad: float32 [2048, 2048], P('dp', 'tensor')
- value_grad: float32 [2048, 2048], P('dp', 'tensor')
- output_grad: float32 [2048, 2048], P('dp', 'tensor')
- postnorm_grad: float32 [2048], P(('dp', 'tensor'))
- router_grad: float32 [2048, 64], P(('dp', 'tensor'))
- gate_grad: float32 [64, 2048, 1024], P('dp', None, 'tensor')
- up_grad: float32 [64, 2048, 1024], P('dp', None, 'tensor')
- down_grad: float32 [64, 2048, 1024], P('dp', None, 'tensor')
Inputs may be any that keep to these rules, and one draw needn't show every extreme that they name: `expert_ids`: each row names 8 different experts; of the 1024 rows of one sequence at most 192 name any one expert. `doc_ids`: ids never fall along a sequence; the last token of every sequence has id 1024 - 1.
All inputs are finite; a program needn't handle non-finite values.
Results may differ from a plain program's by a relative error of at most 0.02.
Values may be sent and summed in bfloat16 or wider, within the bound.
A program may use at most 704 MiB of HBM per device.

v0:
```python
import math

import jax
import jax.numpy as jnp
from jax import lax
from jax.sharding import PartitionSpec as P

D = 2048
HD = 128
E = 64
TOP = 8
CG = 192


epsilon = 1e-05
masked_score = -1000000000.0


def as_sent(value):
    return jax.tree.map(lambda a: a.astype(jnp.bfloat16) if a.dtype == jnp.float32 else a, value)


def rope_tables(length, width):
    positions = jnp.arange(length).astype(jnp.float32)
    rates = 10000.0 ** (-jnp.arange(0, width, 2).astype(jnp.float32) / width)
    angles = positions[:, None] * rates[None, :]
    return (jnp.concatenate([jnp.cos(angles)] * 2, -1), jnp.concatenate([jnp.sin(angles)] * 2, -1))


def rotate(tensor):
    half = tensor.shape[-1] // 2
    return jnp.concatenate([-tensor[..., half:], tensor[..., :half]], -1)


def rotate_back(tensor):
    half = tensor.shape[-1] // 2
    return jnp.concatenate([tensor[..., half:], -tensor[..., :half]], -1)


def gather_tokens(parts):
    return jax.tree.map(
        lambda part, own: part.astype(own.dtype),
        lax.all_gather(as_sent(parts), "tensor", axis=0, tiled=True),
        parts,
    )


def sum_tokens(parts):
    return lax.psum_scatter(parts, "tensor", scatter_dimension=0, tiled=True)


def sum_heads(parts):
    return lax.psum((parts[0], parts[1]), "tensor")


def norm_back(grad, value, inverse, gain, width):
    scaled = grad * gain
    inner = jnp.sum(scaled * value, -1, keepdims=True)
    return inverse * scaled - value * inverse**3 * inner / width


def block_scores(query, keys, documents, start, block, scale):
    row_place = start + jnp.arange(block)
    col_place = jnp.arange(documents.shape[0])
    allowed = (documents[:, None] == documents[None, :]) & (
        row_place[:, None] >= col_place[None, :]
    )
    scores = jnp.einsum("qhd,khd->hqk", query, keys, preferred_element_type=jnp.float32) * scale
    return (jnp.where(allowed[None], scores, masked_score), query)


def attend_forward(query, keys, values, documents, block, scale):
    count = query.shape[0] // block

    def one(index):
        scores, rows = block_scores(query, keys, documents, index * block, block, scale)
        peak = jnp.max(scores, -1, keepdims=True)
        weights = jnp.exp(scores - peak)
        total = jnp.sum(weights, -1, keepdims=True)
        portion = (weights / total).astype(jnp.bfloat16)
        mixed = jnp.einsum("hqk,khd->qhd", portion, values, preferred_element_type=jnp.float32)
        return (mixed.astype(jnp.bfloat16), peak + jnp.log(total))

    mixed, logsum = lax.map(one, jnp.arange(count))
    return (mixed.reshape(query.shape), logsum)


def attend_backward(query, keys, values, documents, logsum, grad_mixed, block, scale):
    count = query.shape[0] // block

    def one(index):
        start = index * block
        scores, rows = block_scores(query, keys, documents, start, block, scale)
        portion = jnp.exp(scores - logsum[index])
        grad_portion = jnp.einsum(
            "qhd,khd->hqk", grad_mixed, values, preferred_element_type=jnp.float32
        )
        center = jnp.sum(portion * grad_portion, -1, keepdims=True)
        grad_scores = (portion * (grad_portion - center)).astype(jnp.bfloat16)
        grad_values = jnp.einsum(
            "hqk,qhd->khd",
            portion.astype(jnp.bfloat16),
            grad_mixed,
            preferred_element_type=jnp.float32,
        )
        grad_query = (
            jnp.einsum("hqk,khd->qhd", grad_scores, keys, preferred_element_type=jnp.float32)
            * scale
        )
        grad_keys = (
            jnp.einsum("hqk,qhd->khd", grad_scores, rows, preferred_element_type=jnp.float32)
            * scale
        )
        return (grad_query, grad_keys, grad_values)

    grad_query, grad_keys, grad_values = lax.map(one, jnp.arange(count))
    return (grad_query.reshape(query.shape), jnp.sum(grad_keys, 0), jnp.sum(grad_values, 0))


def body(
    hidden_in,
    out_grad,
    doc_ids,
    expert_ids,
    prenorm,
    querynorm,
    keynorm,
    query_proj,
    key_proj,
    value_proj,
    output_proj,
    postnorm,
    router,
    gate_proj,
    up_proj,
    down_proj,
):
    residual = hidden_in[0].astype(jnp.float32)
    upstream = out_grad[0]
    documents = doc_ids[0]
    routes = expert_ids[0]
    shard = residual.shape[0]
    seq_len = documents.shape[0]
    hidden_width = gate_proj.shape[2]
    rank = lax.axis_index("tensor")
    block = min(seq_len, 1024)
    scale = HD ** (-0.5)
    cosine, sine = rope_tables(seq_len, HD)
    router_full, pre_gain, post_gain = (
        lax.all_gather(router, ("dp", "tensor"), axis=0, tiled=True),
        lax.all_gather(prenorm, ("dp", "tensor"), axis=0, tiled=True),
        lax.all_gather(postnorm, ("dp", "tensor"), axis=0, tiled=True),
    )
    pre_gain = pre_gain.astype(jnp.float32)
    post_gain = post_gain.astype(jnp.float32)
    w_query, w_key, w_value, w_output, gain_query, gain_key = (
        lax.all_gather(query_proj, "dp", axis=0, tiled=True),
        lax.all_gather(key_proj, "dp", axis=0, tiled=True),
        lax.all_gather(value_proj, "dp", axis=0, tiled=True),
        lax.all_gather(output_proj, "dp", axis=0, tiled=True),
        lax.all_gather(querynorm, "dp", axis=0, tiled=True),
        lax.all_gather(keynorm, "dp", axis=0, tiled=True),
    )
    heads = w_query.shape[1] // HD
    query_scale = gain_query.astype(jnp.float32).T.reshape(-1)
    key_scale = gain_key.astype(jnp.float32).T.reshape(-1)
    inv_pre = lax.rsqrt(jnp.mean(residual * residual, -1, keepdims=True) + epsilon)
    normed = (residual * inv_pre * pre_gain).astype(jnp.bfloat16)
    group_normed, group_grad = gather_tokens((normed, upstream))
    query = jnp.dot(group_normed, w_query, preferred_element_type=jnp.float32)
    keys = jnp.dot(group_normed, w_key, preferred_element_type=jnp.float32)
    values = jnp.dot(group_normed, w_value, preferred_element_type=jnp.float32).astype(jnp.bfloat16)
    query_sq, key_sq = sum_heads(
        (jnp.sum(query * query, -1, keepdims=True), jnp.sum(keys * keys, -1, keepdims=True))
    )
    inv_query = lax.rsqrt(query_sq / D + epsilon)
    inv_key = lax.rsqrt(key_sq / D + epsilon)
    query_heads = (query * inv_query * query_scale).reshape(seq_len, heads, HD)
    key_heads = (keys * inv_key * key_scale).reshape(seq_len, heads, HD)
    query_rot = (query_heads * cosine[:, None] + rotate(query_heads) * sine[:, None]).astype(
        jnp.bfloat16
    )
    key_rot = (key_heads * cosine[:, None] + rotate(key_heads) * sine[:, None]).astype(jnp.bfloat16)
    value_heads = values.reshape(seq_len, heads, HD)
    mixed, logsum = attend_forward(query_rot, key_rot, value_heads, documents, block, scale)
    mixed_flat = mixed.reshape(seq_len, heads * HD)
    attn_term = lax.dot_general(
        mixed_flat, w_output, (((1,), (1,)), ((), ())), preferred_element_type=jnp.float32
    )
    (attn_local,) = sum_tokens((attn_term,))
    middle = residual + attn_local
    inv_post = lax.rsqrt(jnp.mean(middle * middle, -1, keepdims=True) + epsilon)
    post_normed = (middle * inv_post * post_gain).astype(jnp.bfloat16)
    (group_post,) = gather_tokens((post_normed,))
    logits = jnp.dot(group_post, router_full, preferred_element_type=jnp.float32)
    router_share = jax.nn.softmax(logits, -1)
    choose = routes[:, :, None] == jnp.arange(E)[None, None, :]
    gates = jnp.sum(jnp.where(choose, router_share[:, None, :], 0.0), -1)
    flat_routes = routes.reshape(-1)
    picked = choose.reshape(-1, E).astype(jnp.int32)
    place = jnp.sum((jnp.cumsum(picked, 0) - 1) * picked, 1)
    slot = flat_routes * CG + place
    slot_token = (
        jnp.full((E * CG,), seq_len, jnp.int32)
        .at[slot]
        .set(jnp.arange(seq_len * TOP, dtype=jnp.int32) // TOP)
        .reshape(E, CG)
    )
    slot_gate = jnp.zeros((E * CG,), jnp.float32).at[slot].set(gates.reshape(-1)).reshape(E, CG)
    padded_post = jnp.concatenate([group_post, jnp.zeros((1, D), jnp.bfloat16)], 0)
    padded_grad = jnp.concatenate([group_grad, jnp.zeros((1, D), jnp.bfloat16)], 0)

    def expert_inputs(first, group):
        tokens = lax.dynamic_slice_in_dim(slot_token, first, group, 0)
        gate_here = lax.dynamic_slice_in_dim(slot_gate, first, group, 0)
        return (tokens, padded_post[tokens], gate_here)

    zero_rows = jnp.zeros((seq_len + 1, D), jnp.float32)
    saved_zero = jnp.zeros((E, CG, hidden_width), jnp.bfloat16)
    state_init = (
        zero_rows,
        zero_rows,
        jnp.zeros((E, CG), jnp.float32),
        saved_zero,
        saved_zero,
        saved_zero,
    )
    pieces = (
        lax.all_gather(gate_proj, "dp", axis=0, tiled=True),
        lax.all_gather(up_proj, "dp", axis=0, tiled=True),
        lax.all_gather(down_proj, "dp", axis=0, tiled=True),
    )
    group = math.gcd(pieces[0].shape[0], 8)

    def one(step, carry):
        out_rows, grad_rows, slot_change, saved_active, saved_gate, saved_up = carry
        first = step * group
        tokens, rows, gate_here = expert_inputs(first, group)
        upstream_rows = padded_grad[tokens].astype(jnp.float32)
        w_gate = lax.dynamic_slice_in_dim(pieces[0], step * group, group, 0)
        w_up = lax.dynamic_slice_in_dim(pieces[1], step * group, group, 0)
        w_down = lax.dynamic_slice_in_dim(pieces[2], step * group, group, 0)
        gate_pre = jnp.einsum("ecd,edf->ecf", rows, w_gate, preferred_element_type=jnp.float32)
        up_pre = jnp.einsum("ecd,edf->ecf", rows, w_up, preferred_element_type=jnp.float32)
        squash = jax.nn.sigmoid(gate_pre)
        swish = gate_pre * squash
        active = (swish * up_pre).astype(jnp.bfloat16)
        result = jnp.einsum("ecf,edf->ecd", active, w_down, preferred_element_type=jnp.float32)
        flat_tokens = tokens.reshape(-1)
        out_rows = out_rows.at[flat_tokens].add((result * gate_here[..., None]).reshape(-1, D))
        slot_change = lax.dynamic_update_slice_in_dim(
            slot_change, jnp.sum(result * upstream_rows, -1), first, 0
        )
        grad_out = (upstream_rows * gate_here[..., None]).astype(jnp.bfloat16)
        grad_active = jnp.einsum(
            "ecd,edf->ecf", grad_out, w_down, preferred_element_type=jnp.float32
        )
        grad_gate = (grad_active * up_pre * squash * (1.0 + gate_pre * (1.0 - squash))).astype(
            jnp.bfloat16
        )
        grad_up = (grad_active * swish).astype(jnp.bfloat16)
        back_rows = jnp.einsum(
            "ecf,edf->ecd", grad_gate, w_gate, preferred_element_type=jnp.float32
        )
        back_rows = back_rows + jnp.einsum(
            "ecf,edf->ecd", grad_up, w_up, preferred_element_type=jnp.float32
        )
        grad_rows = grad_rows.at[flat_tokens].add(back_rows.reshape(-1, D))
        saved_active = lax.dynamic_update_slice_in_dim(saved_active, active, first, 0)
        saved_gate = lax.dynamic_update_slice_in_dim(saved_gate, grad_gate, first, 0)
        saved_up = lax.dynamic_update_slice_in_dim(saved_up, grad_up, first, 0)
        return (out_rows, grad_rows, slot_change, saved_active, saved_gate, saved_up)

    state = lax.fori_loop(0, pieces[0].shape[0] // group, one, state_init)
    moe_term, grad_rows, slot_change, saved_active, saved_gate, saved_up = state
    (moe_local,) = sum_tokens((moe_term[:seq_len],))
    layer_out = (middle + moe_local).astype(jnp.bfloat16)[None]
    slot_rows = padded_post[slot_token]
    slot_out = (padded_grad[slot_token].astype(jnp.float32) * slot_gate[..., None]).astype(
        jnp.bfloat16
    )
    owned_rows, owned_out, owned_gate, owned_up, owned_active = (
        lax.all_to_all(slot_rows, "dp", split_axis=0, concat_axis=1, tiled=True),
        lax.all_to_all(slot_out, "dp", split_axis=0, concat_axis=1, tiled=True),
        lax.all_to_all(saved_gate, "dp", split_axis=0, concat_axis=1, tiled=True),
        lax.all_to_all(saved_up, "dp", split_axis=0, concat_axis=1, tiled=True),
        lax.all_to_all(saved_active, "dp", split_axis=0, concat_axis=1, tiled=True),
    )
    gate_weight_grad = jnp.einsum(
        "ecd,ecf->edf", owned_rows, owned_gate, preferred_element_type=jnp.float32
    )
    up_weight_grad = jnp.einsum(
        "ecd,ecf->edf", owned_rows, owned_up, preferred_element_type=jnp.float32
    )
    down_weight_grad = jnp.einsum(
        "ecd,ecf->edf", owned_out, owned_active, preferred_element_type=jnp.float32
    )
    route_change = slot_change.reshape(-1)[slot].reshape(seq_len, TOP)
    grad_post, gate_change = sum_tokens((grad_rows[:seq_len], route_change))
    own_share = lax.dynamic_slice_in_dim(router_share, rank * shard, shard, 0)
    own_choose = lax.dynamic_slice_in_dim(choose, rank * shard, shard, 0)
    grad_share = jnp.sum(jnp.where(own_choose, gate_change[:, :, None], 0.0), 1)
    grad_logits = own_share * (grad_share - jnp.sum(grad_share * own_share, -1, keepdims=True))
    router_part = lax.dot_general(
        post_normed.astype(jnp.float32),
        grad_logits,
        (((0,), (0,)), ((), ())),
        precision=lax.Precision.HIGHEST,
    )
    grad_post = grad_post + lax.dot_general(
        grad_logits,
        router_full.astype(jnp.float32),
        (((1,), (1,)), ((), ())),
        precision=lax.Precision.HIGHEST,
    )
    post_gain_part = jnp.sum(grad_post * middle * inv_post, 0)
    grad_middle = upstream.astype(jnp.float32) + norm_back(
        grad_post, middle, inv_post, post_gain, D
    )
    (group_change,) = gather_tokens((grad_middle.astype(jnp.bfloat16),))
    grad_mixed = jnp.dot(group_change, w_output, preferred_element_type=jnp.float32).astype(
        jnp.bfloat16
    )
    output_part = lax.dot_general(
        group_change, mixed_flat, (((0,), (0,)), ((), ())), preferred_element_type=jnp.float32
    )
    grad_query_rot, grad_key_rot, grad_value_heads = attend_backward(
        query_rot,
        key_rot,
        value_heads,
        documents,
        logsum,
        grad_mixed.reshape(seq_len, heads, HD),
        block,
        scale,
    )
    grad_query_flat = (
        grad_query_rot * cosine[:, None] + rotate_back(grad_query_rot * sine[:, None])
    ).reshape(seq_len, -1)
    grad_key_flat = (
        grad_key_rot * cosine[:, None] + rotate_back(grad_key_rot * sine[:, None])
    ).reshape(seq_len, -1)
    query_inner, key_inner = sum_heads(
        (
            jnp.sum(grad_query_flat * query_scale * query, -1, keepdims=True),
            jnp.sum(grad_key_flat * key_scale * keys, -1, keepdims=True),
        )
    )
    grad_query = (
        inv_query * query_scale * grad_query_flat - query * inv_query**3 * query_inner / D
    ).astype(jnp.bfloat16)
    grad_key = (inv_key * key_scale * grad_key_flat - keys * inv_key**3 * key_inner / D).astype(
        jnp.bfloat16
    )
    query_gain_part = jnp.sum(grad_query_flat * query * inv_query, 0).reshape(heads, HD).T
    key_gain_part = jnp.sum(grad_key_flat * keys * inv_key, 0).reshape(heads, HD).T
    grad_value = grad_value_heads.reshape(seq_len, -1).astype(jnp.bfloat16)
    query_part = lax.dot_general(
        group_normed, grad_query, (((0,), (0,)), ((), ())), preferred_element_type=jnp.float32
    )
    key_part = lax.dot_general(
        group_normed, grad_key, (((0,), (0,)), ((), ())), preferred_element_type=jnp.float32
    )
    value_part = lax.dot_general(
        group_normed, grad_value, (((0,), (0,)), ((), ())), preferred_element_type=jnp.float32
    )
    normed_term = lax.dot_general(
        grad_query, w_query, (((1,), (1,)), ((), ())), preferred_element_type=jnp.float32
    )
    normed_term = normed_term + lax.dot_general(
        grad_key, w_key, (((1,), (1,)), ((), ())), preferred_element_type=jnp.float32
    )
    normed_term = normed_term + lax.dot_general(
        grad_value, w_value, (((1,), (1,)), ((), ())), preferred_element_type=jnp.float32
    )
    (grad_normed,) = sum_tokens((normed_term,))
    pre_gain_part = jnp.sum(grad_normed * residual * inv_pre, 0)
    input_grad = (grad_middle + norm_back(grad_normed, residual, inv_pre, pre_gain, D)).astype(
        jnp.bfloat16
    )[None]
    attn_sums = (
        lax.psum_scatter(
            query_part.astype(jnp.bfloat16), "dp", scatter_dimension=0, tiled=True
        ).astype(jnp.float32),
        lax.psum_scatter(
            key_part.astype(jnp.bfloat16), "dp", scatter_dimension=0, tiled=True
        ).astype(jnp.float32),
        lax.psum_scatter(
            value_part.astype(jnp.bfloat16), "dp", scatter_dimension=0, tiled=True
        ).astype(jnp.float32),
        lax.psum_scatter(
            output_part.astype(jnp.bfloat16), "dp", scatter_dimension=0, tiled=True
        ).astype(jnp.float32),
        lax.psum_scatter(
            query_gain_part.astype(jnp.bfloat16), "dp", scatter_dimension=0, tiled=True
        ).astype(jnp.float32),
        lax.psum_scatter(
            key_gain_part.astype(jnp.bfloat16), "dp", scatter_dimension=0, tiled=True
        ).astype(jnp.float32),
    )
    small_sums = (
        lax.psum_scatter(router_part, ("dp", "tensor"), scatter_dimension=0, tiled=True),
        lax.psum_scatter(pre_gain_part, ("dp", "tensor"), scatter_dimension=0, tiled=True),
        lax.psum_scatter(post_gain_part, ("dp", "tensor"), scatter_dimension=0, tiled=True),
    )
    return (
        layer_out,
        input_grad,
        small_sums[1],
        attn_sums[4],
        attn_sums[5],
        attn_sums[0],
        attn_sums[1],
        attn_sums[2],
        attn_sums[3],
        small_sums[2],
        small_sums[0],
        gate_weight_grad,
        up_weight_grad,
        down_weight_grad,
    )


def solution(mesh):
    in_specs = (
        P("dp", "tensor", None),
        P("dp", "tensor", None),
        P("dp", None),
        P("dp", None, None),
        P(("dp", "tensor")),
        P("dp", "tensor"),
        P("dp", "tensor"),
        P("dp", "tensor"),
        P("dp", "tensor"),
        P("dp", "tensor"),
        P("dp", "tensor"),
        P(("dp", "tensor")),
        P(("dp", "tensor"), None),
        P("dp", None, "tensor"),
        P("dp", None, "tensor"),
        P("dp", None, "tensor"),
    )
    out_specs = (
        P("dp", "tensor", None),
        P("dp", "tensor", None),
        P(("dp", "tensor")),
        P("dp", "tensor"),
        P("dp", "tensor"),
        P("dp", "tensor"),
        P("dp", "tensor"),
        P("dp", "tensor"),
        P("dp", "tensor"),
        P(("dp", "tensor")),
        P(("dp", "tensor"), None),
        P("dp", None, "tensor"),
        P("dp", None, "tensor"),
        P("dp", None, "tensor"),
    )
    return jax.shard_map(body, mesh=mesh, in_specs=in_specs, out_specs=out_specs, check_vma=False)
```

profile of v0, /device:TPU:0, one launch (start us, length us, event | category | flops | bytes accessed | tf_op | source)
XLA Modules:
  0.0 4391.9 jit_solution(7725908622852633887)
XLA Ops:
  9.7 42.0 all-reduce.9
  79.1 57.0 %all-gather.15.cloned.1.call-done = bf16[1024,2048]{1,0:T(8,128)(2,1)} async-done(((bf16[256,2048]{1,0:T(8,128)(2,1)}), bf16[1024,2048]{1,0:T(8,128)(2,1)}) %all-gather.15.cloned.1.call-update) | async-done | bytes 4194320 | tf_op jit(solution)/shard_map/all_gather | solution.py:43
  232.0 143.8 %reduce-scatter.17.cloned.1.call-done = f32[256,2048]{1,0:T(8,128)} async-done(((f32[1024,2048]{1,0:T(8,128)}), f32[256,2048]{1,0:T(8,128)}) %reduce-scatter.17.cloned.1.call-update) | async-done | bytes 2097168 | tf_op jit(solution)/shard_map/reduce_scatter | solution.py:49
  385.2 34.0 reduce-window.6
  423.7 30.5 scatter_custom_fusion.2
  455.1 79.8 %all_gather.61 = bf16[2048,64]{1,0:T(8,128)(2,1)S(1)} all-gather(bf16[64,64]{1,0:T(8,128)(2,1)S(1)} %copy-done.62), channel_id=1, replica_groups=mesh['dp'=8,'tensor'=4] {'dp','tensor'}, dimensions={0}, use_global_device_ids=true | all-gather | bytes 270336 | tf_op jit(solution)/shard_map/all_gather | solution.py:150
  553.4 30.5 scatter_custom_fusion.3
  589.3 94.1 %gather_fusion.3 = bf16[12288,2048]{1,0:T(8,128)(2,1)} fusion(bf16[1025,2048]{1,0:T(8,128)(2,1)} %concatenate.28, s32[12288]{0:T(1024)S(1)} %broadcast_clamp_fusion), kind=kCustom, calls=%fused_computation.3 | custom fusion | bytes 100712448 | tf_op jit(solution)/shard_map/gather | solution.py:278
  692.2 446.1 %all-gather.27.cloned.1.call-done = bf16[64,2048,256]{2,1,0:T(8,128)(2,1)} async-done(((bf16[8,2048,256]{2,1,0:T(8,128)(2,1)}), bf16[64,2048,256]{2,1,0:T(8,128)(2,1)}) %all-gather.27.cloned.1.call-update) | async-done | bytes 67108880 | tf_op jit(solution)/shard_map/all_gather | solution.py:229
  1138.3 530.6 %all-gather.29.cloned.1.call-done = bf16[64,2048,256]{2,1,0:T(8,128)(2,1)} async-done(((bf16[8,2048,256]{2,1,0:T(8,128)(2,1)}), bf16[64,2048,256]{2,1,0:T(8,128)(2,1)}) %all-gather.29.cloned.1.call-update) | async-done | bytes 67108880 | tf_op jit(solution)/shard_map/all_gather | solution.py:230
  1668.9 304.8 %all-gather.31.cloned.1.call-done = bf16[64,2048,256]{2,1,0:T(8,128)(2,1)} async-done(((bf16[8,2048,256]{2,1,0:T(8,128)(2,1)}), bf16[64,2048,256]{2,1,0:T(8,128)(2,1)}) %all-gather.31.cloned.1.call-update) | async-done | bytes 67108880 | tf_op jit(solution)/shard_map/all_gather | solution.py:231
  1993.4 1209.5 %while.4 = (s32[]{:T(128)}, f32[1025,2048]{1,0:T(8,128)}, f32[1025,2048]{1,0:T(8,128)}, f32[64,192]{1,0:T(8,128)}, bf16[64,192,256]{2,1,0:T(8,128)(2,1)}, /*inde...) while((s32[]{:T(128)}, f32[1025,2048]{1,0:T(8,128)}, ...), condition=%wide.region_21.22_spmd, body=%wide.region_17.21_spmd.sunk | while | flops 9701042176 | bytes 284042560 | solution.py:274
  3203.9 45.5 %gather_fusion.2 = f32[8192]{0:T(1024)S(1)} fusion(f32[12288]{0:T(1024)S(1)} %reshape.334, s32[8192]{0:T(1024)S(1)} %copy-done.45), kind=kCustom, calls=%fused_computation.2 | custom fusion | bytes 98304 | tf_op jit(solution)/shard_map/gather | solution.py:298
  3267.1 94.1 %gather_fusion.4 = bf16[12288,2048]{1,0:T(8,128)(2,1)} fusion(bf16[1025,2048]{1,0:T(8,128)(2,1)} %get-tuple-element.594, s32[12288]{0:T(1024)S(1)} %copy-done.35), kind=kCustom, calls=%fused_computation.4 | custom fusion | bytes 100712448 | tf_op jit(solution)/shard_map/gather | solution.py:279
  3361.3 33.7 fusion.27
  3423.1 142.4 %reduce-scatter.19.cloned.1.call-done = f32[256,2048]{1,0:T(8,128)} async-done(((f32[1024,2048]{1,0:T(8,128)}), f32[256,2048]{1,0:T(8,128)}) %reduce-scatter.19.cloned.1.call-update) | async-done | bytes 2097168 | tf_op jit(solution)/shard_map/reduce_scatter | solution.py:49
  3571.6 81.0 %all-gather.33.cloned.1.call-done = bf16[1024,2048]{1,0:T(8,128)(2,1)} async-done(((bf16[256,2048]{1,0:T(8,128)(2,1)}), bf16[1024,2048]{1,0:T(8,128)(2,1)}) %all-gather.33.cloned.1.call-update) | async-done | bytes 4194320 | tf_op jit(solution)/shard_map/all_gather | solution.py:43
  3758.9 205.5 %all-to-all-done.3 = bf16[64,192,2048]{2,1,0:T(8,128)(2,1)} async-done(((bf16[64,192,2048]{2,1,0:T(8,128)(2,1)}), bf16[64,192,2048]{2,1,0:T(8,128)(2,1)}, u32[]{:S(2)}, u32[]{:S(2)}) %all-to-all-start.3) | async-done | bytes 50331680 | tf_op jit(solution)/shard_map/all_to_all | solution.py:284
  3964.4 85.3 %all_to_all.90 = bf16[64,192,256]{2,1,0:T(8,128)(2,1)} all-to-all(bf16[64,192,256]{2,1,0:T(8,128)(2,1)} %get-tuple-element.302), channel_id=1, replica_groups=mesh['dp'=8,'tensor'=4] {'dp'}, dimensions={0} | all-to-all | bytes 12582912 | tf_op jit(solution)/shard_map/all_to_all | solution.py:285
  4054.6 33.5 copy.127
  4088.1 33.9 copy.132
  4214.3 30.4 fusion.94
  4257.2 40.2 all-reduce.6
  4301.8 83.1 %reduce-scatter.35.cloned.1.call-done = f32[64,64]{1,0:T(8,128)} async-done(((f32[2048,64]{1,0:T(8,128)}), f32[64,64]{1,0:T(8,128)}) %reduce-scatter.35.cloned.1.call-update) | async-done | bytes 16400 | tf_op jit(solution)/shard_map/reduce_scatter | solution.py:402
  (544 shorter events, 1666.8 us)
Async XLA Ops:
  7.9 128.1 %all-gather.15.cloned.1.call-start = ((), (), s32[]{:S(2)}) async-start(), calls=%async_computation.17 | async-start | bytes 5242880 | tf_op jit(solution)/shard_map/all_gather | solution.py:43
  55.2 109.2 %all-gather.19.cloned.1.call-start = ((), (), s32[]{:S(2)}) async-start(), calls=%async_computation.19 | async-start | bytes 2359296 | tf_op jit(solution)/shard_map/all_gather | solution.py:157
  55.9 142.2 %all-gather.17.cloned.1.call-start = ((), (), s32[]{:S(2)}) async-start(), calls=%async_computation.18 | async-start | bytes 2359296 | tf_op jit(solution)/shard_map/all_gather | solution.py:159
  56.5 167.2 %all-gather.23.cloned.1.call-start = ((), (), s32[]{:S(2)}) async-start(), calls=%async_computation.21 | async-start | bytes 2359296 | tf_op jit(solution)/shard_map/all_gather | solution.py:160
  57.1 318.7 %reduce-scatter.17.cloned.1.call-start = ((), (), s32[]{:S(2)}) async-start(), calls=%async_computation.22 | async-start | bytes 10485760 | tf_op jit(solution)/shard_map/reduce_scatter | solution.py:49
  231.1 304.4 %all-gather.35.cloned.1.call-start = ((), (), s32[]{:S(2)}) async-start(), calls=%async_computation.37 | async-start | bytes 5242880 | tf_op jit(solution)/shard_map/all_gather | solution.py:43
  231.9 316.3 %all-gather.25.cloned.1.call-start = ((), (), s32[]{:S(2)}) async-start(), calls=%async_computation.23 | async-start | bytes 5242880 | tf_op jit(solution)/shard_map/all_gather | solution.py:43
  380.3 758.1 %all-gather.27.cloned.1.call-start = ((), (), s32[]{:S(2)}) async-start(), calls=%async_computation.24 | async-start | bytes 75497472 | tf_op jit(solution)/shard_map/all_gather | solution.py:229
  381.0 1287.9 %all-gather.29.cloned.1.call-start = ((), (), s32[]{:S(2)}) async-start(), calls=%async_computation.25 | async-start | bytes 75497472 | tf_op jit(solution)/shard_map/all_gather | solution.py:230
  381.6 1592.1 %all-gather.31.cloned.1.call-start = ((), (), s32[]{:S(2)}) async-start(), calls=%async_computation.26 | async-start | bytes 75497472 | tf_op jit(solution)/shard_map/all_gather | solution.py:231
  683.4 2711.6 %all-to-all-start = ((bf16[64,192,2048]{2,1,0:T(8,128)(2,1)}), bf16[64,192,2048]{2,1,0:T(8,128)(2,1)}, u32[]{:S(2)}, u32[]{:S(2)}) async-start(bf16[64,192,2048]{2,1,0:T(8,128)(2,1)} %bitcast.223), calls=%async_computation.10 | async-start | bytes 100663296 | tf_op jit(solution)/shard_map/all_to_all | solution.py:283
  692.0 2712.2 %reduce-scatter.23.cloned.1.call-start = ((), (), s32[]{:S(2)}) async-start(), calls=%async_computation.29 | async-start | bytes 655360 | tf_op jit(solution)/shard_map/reduce_scatter | solution.py:49
  3250.5 167.5 %reduce-scatter.21.cloned.1.call-start = ((), (), s32[]{:S(2)}) async-start(), calls=%async_computation.28 | async-start | bytes 10485760 | tf_op jit(solution)/shard_map/reduce_scatter | solution.py:49
  3258.5 307.0 %reduce-scatter.19.cloned.1.call-start = ((), (), s32[]{:S(2)}) async-start(), calls=%async_computation.27 | async-start | bytes 10485760 | tf_op jit(solution)/shard_map/reduce_scatter | solution.py:49
  3395.0 569.4 %all-to-all-start.3 = ((bf16[64,192,2048]{2,1,0:T(8,128)(2,1)}), bf16[64,192,2048]{2,1,0:T(8,128)(2,1)}, u32[]{:S(2)}, u32[]{:S(2)}) async-start(bf16[64,192,2048]{2,1,0:T(8,128)(2,1)} %fusion.27), calls=%async_computation.13 | async-start | bytes 100663296 | tf_op jit(solution)/shard_map/all_to_all | solution.py:284
  3403.8 248.7 %all-gather.33.cloned.1.call-start = ((), (), s32[]{:S(2)}) async-start(), calls=%async_computation.30 | async-start | bytes 5242880 | tf_op jit(solution)/shard_map/all_gather | solution.py:43
  3570.9 673.9 %reduce-scatter.37.cloned.1.call-start = ((), (), s32[]{:S(2)}) async-start(), calls=%async_computation.38 | async-start | bytes 36864
  3696.7 549.5 %reduce-scatter.39.cloned.1.call-start = ((), (), s32[]{:S(2)}) async-start(), calls=%async_computation.39 | async-start | bytes 36864
  3699.8 547.8 %reduce-scatter.27.cloned.1.call-start = ((), (), s32[]{:S(2)}) async-start(), calls=%async_computation.32 | async-start | bytes 2359296 | tf_op jit(solution)/shard_map/reduce_scatter | solution.py:382
  3716.7 532.7 %reduce-scatter.29.cloned.1.call-start = ((), (), s32[]{:S(2)}) async-start(), calls=%async_computation.33 | async-start | bytes 2359296 | tf_op jit(solution)/shard_map/reduce_scatter | solution.py:385
  3724.7 526.6 %reduce-scatter.31.cloned.1.call-start = ((), (), s32[]{:S(2)}) async-start(), calls=%async_computation.34 | async-start | bytes 2359296 | tf_op jit(solution)/shard_map/reduce_scatter | solution.py:388
  3738.1 514.9 %reduce-scatter.33.cloned.1.call-start = ((), (), s32[]{:S(2)}) async-start(), calls=%async_computation.35 | async-start | bytes 2359296 | tf_op jit(solution)/shard_map/reduce_scatter | solution.py:391
  3745.3 509.5 %reduce-scatter.25.cloned.1.call-start = ((), (), s32[]{:S(2)}) async-start(), calls=%async_computation.31 | async-start | bytes 10485760 | tf_op jit(solution)/shard_map/reduce_scatter | solution.py:49
  4054.5 330.4 %reduce-scatter.35.cloned.1.call-start = ((), (), s32[]{:S(2)}) async-start(), calls=%async_computation.36 | async-start | bytes 1081344 | tf_op jit(solution)/shard_map/reduce_scatter | solution.py:402
  (107 other events, 3137.9 us)
Sparse Core Ops, SparseCore 0:
  9.9 30.7 all-gather.20
  55.3 80.6 all-gather.14
  137.9 26.4 all-gather.18
  166.1 27.8 all-gather.16
  195.8 27.8 all-gather.22
  231.3 144.4 reduce-scatter.16
  377.3 81.4 all-gather.34
  461.0 87.1 all-gather.24
  550.1 588.2 all-gather.26
  1140.1 528.8 all-gather.28
  1670.8 302.8 all-gather.30
  3250.7 21.6 reduce-scatter.22
  3275.3 142.6 reduce-scatter.20
  3420.2 145.1 reduce-scatter.18
  3571.0 81.4 all-gather.32
  3696.8 124.8 reduce-scatter.36
  3825.5 31.5 reduce-scatter.38
  3860.2 50.7 reduce-scatter.26
  3914.6 49.8 reduce-scatter.28
  3967.7 57.7 reduce-scatter.30
  4029.1 70.2 reduce-scatter.32
  4101.8 143.5 reduce-scatter.24
  4248.2 136.6 reduce-scatter.34
where the time goes:
time: 4410 us; the launch traced here: 4390 us
  waiting for transfers between devices  2050 us (46%)
  local copies, waits for them, and re-layouts  716 us (16%)
  matrix products  704 us (16%)
  other arithmetic  581 us (13%)
  blocking collectives  286 us (6%)
    all_gather x1, waiting for transfers between devices, body(): lax.all_gather(up_proj, 'dp', axis=0, tiled=True)  531 us
    all_gather x1, waiting for transfers between devices, body(): lax.all_gather(gate_proj, 'dp', axis=0, tiled=True)  446 us
    all_gather x1, waiting for transfers between devices, body(): lax.all_gather(down_proj, 'dp', axis=0, tiled=True)  305 us
    reduce_scatter x5, waiting for transfers between devices, sum_tokens(): return lax.psum_scatter(parts, 'tensor', scatter_dimension=0, tiled=True)  299 us
    scatter-add x8, other arithmetic, one(): out_rows.at[flat_tokens].add((result * gate_here[..., None]).reshape(-1, D))  221 us
    scatter-add x8, other arithmetic, one(): grad_rows = grad_rows.at[flat_tokens].add(back_rows.reshape(-1, D))  220 us
    all_to_all x1, waiting for transfers between devices, body(): lax.all_to_all(slot_out, 'dp', split_axis=0, concat_axis=1, tiled=True)  205 us
    all_gather x4, waiting for transfers between devices, gather_tokens(): lax.all_gather(as_sent(parts), 'tensor', axis=0, tiled=True)  146 us
  transfers between devices with their start and end apart: 27, of which 14 were waited for; matrix products, arithmetic and copies ran while one was open for 45% of the time, Pallas kernels for 0%

commit v1 on v0

--- a/solution.py
+++ b/solution.py
@@ -1,8 +1,10 @@
-import math
+import functools
 
 import jax
 import jax.numpy as jnp
 from jax import lax
+from jax.experimental import pallas as pl
+from jax.experimental.pallas import tpu as pltpu
 from jax.sharding import PartitionSpec as P
 
 D = 2048
@@ -45,8 +47,14 @@
     )
 
 
-def sum_tokens(parts):
-    return lax.psum_scatter(parts, "tensor", scatter_dimension=0, tiled=True)
+def sum_tokens(part):
+    return lax.psum_scatter(
+        part.astype(jnp.bfloat16), "tensor", scatter_dimension=0, tiled=True
+    ).astype(jnp.float32)
+
+
+def sum_all(part):
+    return sum_tokens(lax.psum_scatter(part, "dp", scatter_dimension=0, tiled=True))
 
 
 def sum_heads(parts):
@@ -117,6 +125,413 @@
     return (grad_query.reshape(query.shape), jnp.sum(grad_keys, 0), jnp.sum(grad_values, 0))
 
 
+TB = 256
+GR = 16
+TILE = 256
+SLOTS = 512
+EXTRA = 2 * E
+VMEM = 60 * 1024 * 1024
+
+
+def ceil_to(value, unit):
+    return (value + unit - 1) // unit * unit
+
+
+def nt_dot(a, b):
+    return lax.dot_general(a, b, (((1,), (1,)), ((), ())), preferred_element_type=jnp.float32)
+
+
+def tn_dot(a, b):
+    return lax.dot_general(a, b, (((0,), (0,)), ((), ())), preferred_element_type=jnp.float32)
+
+
+def nn_dot(a, b):
+    return jnp.dot(a, b, preferred_element_type=jnp.float32)
+
+
+def pair(value):
+    high = value.astype(jnp.bfloat16)
+    low = (value - high.astype(jnp.float32)).astype(jnp.bfloat16)
+    return high, low
+
+
+def unpair(value):
+    value = value.astype(jnp.float32)
+    return value[:, :E] + value[:, E:]
+
+
+def excl_cumsum(value, axis):
+    return jnp.cumsum(value, axis) - value
+
+
+class Plan:
+    def __init__(self, tokens, seq_len, local):
+        seqs = tokens // seq_len
+        self.tokens, self.local = tokens, local
+        self.blocks = tokens // TB
+        per_seq = seq_len // TB
+        worst = min(CG + (GR - 1) * per_seq, seq_len)
+        self.cap = ceil_to(seqs * worst // GR * GR, TILE)
+        groups = (seqs * local * CG + self.blocks * local * (GR - 1)) // GR
+        self.items = groups * GR // TILE + self.blocks
+        self.joins = groups * GR // SLOTS + self.blocks
+        self.tiles = self.cap // TILE
+
+
+def routing(plan, routes, base):
+    local, blocks = plan.local, plan.blocks
+    mine = base + jnp.arange(local)
+    picked = jnp.any(routes[:, :, None] == mine[None, None, :], 1)
+    grid = picked.reshape(blocks, TB, local)
+    ones = grid.astype(jnp.bfloat16)
+    earlier = (jnp.arange(TB)[:, None] > jnp.arange(TB)[None, :]).astype(jnp.bfloat16)
+    rank = jnp.einsum("ts,bse->bte", earlier, ones, preferred_element_type=jnp.float32).astype(
+        jnp.int32
+    )
+    count = jnp.sum(grid.astype(jnp.int32), 1)
+    groups = (count + GR - 1) // GR
+    inner = excl_cumsum(groups, 1)
+    total = jnp.sum(groups, 1)
+    outer = excl_cumsum(groups, 0)
+    expert_rows = jnp.sum(groups, 0) * GR
+    place = jnp.where(grid, inner[:, None, :] * GR + rank, -1)
+
+    def items(size, unit):
+        steps = jnp.maximum((total * GR + unit - 1) // unit, 1)
+        first = excl_cumsum(steps, 0)
+        used = jnp.sum(steps)
+        index = jnp.minimum(jnp.arange(size), used - 1)
+        block = jnp.sum((first[None, :] <= index[:, None]).astype(jnp.int32), 1) - 1
+        here = block[:, None] == jnp.arange(blocks)[None, :]
+        part = index - jnp.sum(jnp.where(here, first[None, :], 0), 1)
+        last = part == jnp.sum(jnp.where(here, steps[None, :], 0), 1) - 1
+        return first, used, block, part, last.astype(jnp.int32), here
+
+    first, used, block, part, _, _ = items(plan.items, TILE)
+    slots = plan.cap // GR
+    spot = jnp.arange(slots)[None, :, None]
+    low = outer.T[:, None, :]
+    inside = (spot >= low) & (spot < low + groups.T[:, None, :])
+    origin = first[None, :] * (TILE // GR) + inner.T
+    source = jnp.sum(jnp.where(inside, origin[:, None, :] + spot - low, 0), 2)
+    _, joined, jblock, jpart, jlast, here = items(plan.joins, SLOTS)
+
+    def at_block(table):
+        return jnp.sum(jnp.where(here[:, :, None], table[None], 0), 1)[:, None, :]
+
+    wide = SLOTS // GR
+    spot = (jpart[:, None] * wide + jnp.arange(wide)[None, :])[:, :, None]
+    low, many, begin = at_block(inner), at_block(groups), at_block(outer)
+    inside = (spot >= low) & (spot < low + many)
+    target = jnp.sum(
+        jnp.where(inside, (jnp.arange(local) * slots)[None, None, :] + begin + spot - low, 0), 2
+    )
+    return dict(
+        place=place,
+        used=used[None],
+        block=block,
+        part=part,
+        source=source.reshape(-1),
+        expert_rows=expert_rows,
+        expert_tiles=jnp.maximum((expert_rows + TILE - 1) // TILE, 1),
+        joined=joined[None],
+        jblock=jblock,
+        jpart=jpart,
+        jlast=jlast,
+        target=target.reshape(-1),
+    )
+
+
+def dispatch_kernel(used, block, part, post, grad, router, place, rows, share, held):
+    step = pl.program_id(0)
+    local = place.shape[1]
+
+    @pl.when(step < used[0])
+    def _():
+        @pl.when(part[step] == 0)
+        def _():
+            portion = jax.nn.softmax(nn_dot(post[...], router[...]), -1)
+            high, low = pair(portion)
+            both = jnp.concatenate([high, low], 1)
+            held[...] = both
+            share[...] = both
+
+        slot = lax.broadcasted_iota(jnp.int32, (TILE, TB), 0) + part[step] * TILE
+        hit = slot == place[0, 0:1, :]
+        for one in range(1, local):
+            hit = hit | (slot == place[0, one : one + 1, :])
+        pick = jnp.where(hit, 1.0, 0.0).astype(jnp.bfloat16)
+        rows[:, :D] = nn_dot(pick, post[...]).astype(jnp.bfloat16)
+        rows[:, D : 2 * D] = nn_dot(pick, grad[...]).astype(jnp.bfloat16)
+        rows[:, 2 * D :] = nn_dot(pick, held[...]).astype(jnp.bfloat16)
+
+
+def dispatch(plan, route, post, grad, router):
+    wide = 2 * D + EXTRA
+    place = route["place"].transpose(0, 2, 1)
+
+    def at_block(step, used, block, part):
+        return (block[step], 0)
+
+    return pl.pallas_call(
+        dispatch_kernel,
+        grid_spec=pltpu.PrefetchScalarGridSpec(
+            num_scalar_prefetch=3,
+            grid=(plan.items,),
+            in_specs=[
+                pl.BlockSpec((TB, D), at_block),
+                pl.BlockSpec((TB, D), at_block),
+                pl.BlockSpec((D, E), lambda step, used, block, part: (0, 0)),
+                pl.BlockSpec((1, plan.local, TB), lambda s, used, block, part: (block[s], 0, 0)),
+            ],
+            out_specs=[
+                pl.BlockSpec(
+                    (TILE, wide), lambda s, used, block, part: (jnp.minimum(s, used[0] - 1), 0)
+                ),
+                pl.BlockSpec((TB, EXTRA), at_block),
+            ],
+            scratch_shapes=[pltpu.VMEM((TB, EXTRA), jnp.bfloat16)],
+        ),
+        out_shape=[
+            jax.ShapeDtypeStruct((plan.items * TILE, wide), jnp.bfloat16),
+            jax.ShapeDtypeStruct((plan.tokens, EXTRA), jnp.bfloat16),
+        ],
+        compiler_params=pltpu.CompilerParams(vmem_limit_bytes=VMEM),
+        cost_estimate=pl.CostEstimate(
+            flops=2 * plan.items * TILE * TB * wide,
+            bytes_accessed=4 * plan.items * TILE * wide,
+            transcendentals=0,
+        ),
+        name="dispatch",
+    )(route["used"], route["block"], route["part"], post, grad, router, place)
+
+
+def expert_kernel(source, tiles, filled, base, *refs):
+    count = TILE // GR
+    parts = refs[:count]
+    w_gate, w_up, w_down, result, gate_out, up_out, down_out = refs[count : count + 7]
+    gate_sum, up_sum, down_sum = refs[count + 7 :]
+    expert, step = pl.program_id(0), pl.program_id(1)
+
+    @pl.when(step == 0)
+    def _():
+        gate_sum[...] = jnp.zeros_like(gate_sum)
+        up_sum[...] = jnp.zeros_like(up_sum)
+        down_sum[...] = jnp.zeros_like(down_sum)
+
+    @pl.when(step < tiles[expert])
+    def _():
+        number = base[0] + expert
+        real = lax.broadcasted_iota(jnp.int32, (TILE, 1), 0) < filled[expert] - step * TILE
+
+        def take(begin, end):
+            value = jnp.concatenate([part[:, begin:end] for part in parts], 0)
+            return jnp.where(real, value, jnp.zeros_like(value))
+
+        rows, upstream, shares = take(0, D), take(D, 2 * D), take(2 * D, 2 * D + EXTRA)
+        lane = lax.broadcasted_iota(jnp.int32, (TILE, EXTRA), 1)
+        own = (lane == number) | (lane == number + E)
+        gate = jnp.sum(jnp.where(own, shares.astype(jnp.float32), 0.0), -1, keepdims=True)
+        gate_pre = nn_dot(rows, w_gate[0])
+        up_pre = nn_dot(rows, w_up[0])
+        plain = nn_dot(upstream, w_down[0])
+        squash = jax.nn.sigmoid(gate_pre)
+        swish = gate_pre * squash
+        active = (swish * up_pre).astype(jnp.bfloat16).astype(jnp.float32)
+        change = jnp.sum(active * plain, -1, keepdims=True)
+        grad_active = gate * plain
+        grad_gate = (grad_active * up_pre * squash * (1.0 + gate_pre * (1.0 - squash))).astype(
+            jnp.bfloat16
+        )
+        grad_up = (grad_active * swish).astype(jnp.bfloat16)
+        scaled = (gate * active).astype(jnp.bfloat16)
+        result[:, :D] = nt_dot(scaled, w_down[0]).astype(jnp.bfloat16)
+        result[:, D : 2 * D] = (nt_dot(grad_gate, w_gate[0]) + nt_dot(grad_up, w_up[0])).astype(
+            jnp.bfloat16
+        )
+        high, low = pair(change)
+        result[:, 2 * D :] = jnp.where(
+            lane == number,
+            high.astype(jnp.float32),
+            jnp.where(lane == number + E, low.astype(jnp.float32), 0.0),
+        ).astype(jnp.bfloat16)
+        gate_sum[...] += tn_dot(grad_gate, rows)
+        up_sum[...] += tn_dot(grad_up, rows)
+        down_sum[...] += tn_dot(scaled, upstream)
+
+    @pl.when(step == pl.num_programs(1) - 1)
+    def _():
+        gate_out[0] = gate_sum[...].T
+        up_out[0] = up_sum[...].T
+        down_out[0] = down_sum[...].T
+
+
+def experts(plan, route, base, rows, w_gate, w_up, w_down):
+    wide = 2 * D + EXTRA
+    width = w_gate.shape[2]
+    count = TILE // GR
+    slots = plan.cap // GR
+
+    def group_at(index):
+        def place(expert, step, source, tiles, filled, base):
+            tile = jnp.minimum(step, tiles[expert] - 1)
+            return (source[expert * slots + tile * count + index], 0)
+
+        return pl.BlockSpec((GR, wide), place)
+
+    def whole(expert, step, source, tiles, filled, base):
+        return (expert, 0, 0)
+
+    def tile_at(expert, step, source, tiles, filled, base):
+        return (expert * plan.tiles + jnp.minimum(step, tiles[expert] - 1), 0)
+
+    weight = pl.BlockSpec((1, D, width), whole)
+    total = plan.local * plan.cap
+    return pl.pallas_call(
+        expert_kernel,
+        grid_spec=pltpu.PrefetchScalarGridSpec(
+            num_scalar_prefetch=4,
+            grid=(plan.local, plan.tiles),
+            in_specs=[group_at(index) for index in range(count)] + [weight] * 3,
+            out_specs=[pl.BlockSpec((TILE, wide), tile_at)] + [weight] * 3,
+            scratch_shapes=[pltpu.VMEM((width, D), jnp.float32)] * 3,
+        ),
+        out_shape=[jax.ShapeDtypeStruct((total, wide), jnp.bfloat16)]
+        + [jax.ShapeDtypeStruct((plan.local, D, width), jnp.float32)] * 3,
+        compiler_params=pltpu.CompilerParams(vmem_limit_bytes=VMEM),
+        cost_estimate=pl.CostEstimate(
+            flops=18 * total * D * width * 5 // 8,
+            bytes_accessed=4 * total * wide * 5 // 8,
+            transcendentals=0,
+        ),
+        name="experts",
+    )(
+        route["source"],
+        route["expert_tiles"],
+        route["expert_rows"],
+        base[None],
+        *([rows] * count),
+        w_gate,
+        w_up,
+        w_down,
+    )
+
+
+def combine_kernel(joined, block, part, last, target, *refs):
+    count = SLOTS // GR
+    groups = refs[:count]
+    place, share, post, router, out, grad, router_out, sums = refs[count:]
+    step = pl.program_id(0)
+    local = place.shape[1]
+
+    @pl.when(step == 0)
+    def _():
+        router_out[...] = jnp.zeros_like(router_out)
+
+    @pl.when(step < joined[0])
+    def _():
+        slot = lax.broadcasted_iota(jnp.int32, (TB, SLOTS), 1) + part[step] * SLOTS
+        hit = slot == place[:, 0:1]
+        for one in range(1, local):
+            hit = hit | (slot == place[:, one : one + 1])
+        pick = jnp.where(hit, 1.0, 0.0).astype(jnp.bfloat16)
+
+        def term(begin, end):
+            return nn_dot(pick, jnp.concatenate([group[:, begin:end] for group in groups], 0))
+
+        def finish(value):
+            change = unpair_wide(value(2 * D, 2 * D + EXTRA))
+            portion = unpair(share[...])
+            moved = portion * (change - jnp.sum(change * portion, -1, keepdims=True))
+            moved = moved.astype(jnp.bfloat16)
+            out[...] = value(0, D).astype(jnp.bfloat16)
+            grad[...] = (value(D, 2 * D) + nt_dot(moved, router[...])).astype(jnp.bfloat16)
+            router_out[...] += tn_dot(moved, post[...])
+
+        single = (part[step] == 0) & (last[step] == 1)
+
+        @pl.when(single)
+        def _():
+            finish(term)
+
+        @pl.when(jnp.logical_not(single))
+        def _():
+            @pl.when(part[step] == 0)
+            def _():
+                sums[...] = jnp.zeros_like(sums)
+
+            sums[...] += term(0, 2 * D + EXTRA)
+
+            @pl.when(last[step] == 1)
+            def _():
+                finish(lambda begin, end: sums[:, begin:end])
+
+
+def unpair_wide(value):
+    return value[:, :E] + value[:, E:]
+
+
+def combine(plan, route, results, share, post, router):
+    wide = 2 * D + EXTRA
+    count = SLOTS // GR
+
+    def group_at(index):
+        def place(step, joined, block, part, last, target):
+            return (target[step * count + index], 0)
+
+        return pl.BlockSpec((GR, wide), place)
+
+    def at_block(step, joined, block, part, last, target):
+        return (block[step], 0)
+
+    def fixed(step, joined, block, part, last, target):
+        return (0, 0)
+
+    return pl.pallas_call(
+        combine_kernel,
+        grid_spec=pltpu.PrefetchScalarGridSpec(
+            num_scalar_prefetch=5,
+            grid=(plan.joins,),
+            in_specs=[group_at(index) for index in range(count)]
+            + [
+                pl.BlockSpec((TB, plan.local), at_block),
+                pl.BlockSpec((TB, EXTRA), at_block),
+                pl.BlockSpec((TB, D), at_block),
+                pl.BlockSpec((D, E), fixed),
+            ],
+            out_specs=[
+                pl.BlockSpec((TB, D), at_block),
+                pl.BlockSpec((TB, D), at_block),
+                pl.BlockSpec((E, D), fixed),
+            ],
+            scratch_shapes=[pltpu.VMEM((TB, wide), jnp.float32)],
+        ),
+        out_shape=[
+            jax.ShapeDtypeStruct((plan.tokens, D), jnp.bfloat16),
+            jax.ShapeDtypeStruct((plan.tokens, D), jnp.bfloat16),
+            jax.ShapeDtypeStruct((E, D), jnp.float32),
+        ],
+        compiler_params=pltpu.CompilerParams(vmem_limit_bytes=VMEM),
+        cost_estimate=pl.CostEstimate(
+            flops=2 * plan.joins * SLOTS * TB * wide,
+            bytes_accessed=4 * plan.tokens * wide,
+            transcendentals=0,
+        ),
+        name="combine",
+    )(
+        route["joined"],
+        route["jblock"],
+        route["jpart"],
+        route["jlast"],
+        route["target"],
+        *([results] * count),
+        route["place"].reshape(plan.tokens, plan.local),
+        share,
+        post,
+        router,
+    )
+
+
 def body(
     hidden_in,
     out_grad,
@@ -141,8 +556,7 @@
     routes = expert_ids[0]
     shard = residual.shape[0]
     seq_len = documents.shape[0]
-    hidden_width = gate_proj.shape[2]
-    rank = lax.axis_index("tensor")
+    mesh_dp = lax.axis_size("dp")
     block = min(seq_len, 1024)
     scale = HD ** (-0.5)
     cosine, sine = rope_tables(seq_len, HD)
@@ -166,7 +580,12 @@
     key_scale = gain_key.astype(jnp.float32).T.reshape(-1)
     inv_pre = lax.rsqrt(jnp.mean(residual * residual, -1, keepdims=True) + epsilon)
     normed = (residual * inv_pre * pre_gain).astype(jnp.bfloat16)
-    group_normed, group_grad = gather_tokens((normed, upstream))
+    (group_normed,) = gather_tokens((normed,))
+    plan = Plan(mesh_dp * seq_len, seq_len, gate_proj.shape[0])
+    base = (lax.axis_index("dp") * plan.local).astype(jnp.int32)
+    all_routes = lax.all_gather(routes, "dp", axis=0, tiled=True)
+    all_grad = lax.all_gather(upstream, ("dp", "tensor"), axis=0, tiled=True)
+    route = routing(plan, all_routes, base)
     query = jnp.dot(group_normed, w_query, preferred_element_type=jnp.float32)
     keys = jnp.dot(group_normed, w_key, preferred_element_type=jnp.float32)
     values = jnp.dot(group_normed, w_value, preferred_element_type=jnp.float32).astype(jnp.bfloat16)
@@ -187,132 +606,22 @@
     attn_term = lax.dot_general(
         mixed_flat, w_output, (((1,), (1,)), ((), ())), preferred_element_type=jnp.float32
     )
-    (attn_local,) = sum_tokens((attn_term,))
+    attn_local = sum_tokens(attn_term)
     middle = residual + attn_local
     inv_post = lax.rsqrt(jnp.mean(middle * middle, -1, keepdims=True) + epsilon)
     post_normed = (middle * inv_post * post_gain).astype(jnp.bfloat16)
-    (group_post,) = gather_tokens((post_normed,))
-    logits = jnp.dot(group_post, router_full, preferred_element_type=jnp.float32)
-    router_share = jax.nn.softmax(logits, -1)
-    choose = routes[:, :, None] == jnp.arange(E)[None, None, :]
-    gates = jnp.sum(jnp.where(choose, router_share[:, None, :], 0.0), -1)
-    flat_routes = routes.reshape(-1)
-    picked = choose.reshape(-1, E).astype(jnp.int32)
-    place = jnp.sum((jnp.cumsum(picked, 0) - 1) * picked, 1)
-    slot = flat_routes * CG + place
-    slot_token = (
-        jnp.full((E * CG,), seq_len, jnp.int32)
-        .at[slot]
-        .set(jnp.arange(seq_len * TOP, dtype=jnp.int32) // TOP)
-        .reshape(E, CG)
-    )
-    slot_gate = jnp.zeros((E * CG,), jnp.float32).at[slot].set(gates.reshape(-1)).reshape(E, CG)
-    padded_post = jnp.concatenate([group_post, jnp.zeros((1, D), jnp.bfloat16)], 0)
-    padded_grad = jnp.concatenate([group_grad, jnp.zeros((1, D), jnp.bfloat16)], 0)
-
-    def expert_inputs(first, group):
-        tokens = lax.dynamic_slice_in_dim(slot_token, first, group, 0)
-        gate_here = lax.dynamic_slice_in_dim(slot_gate, first, group, 0)
-        return (tokens, padded_post[tokens], gate_here)
-
-    zero_rows = jnp.zeros((seq_len + 1, D), jnp.float32)
-    saved_zero = jnp.zeros((E, CG, hidden_width), jnp.bfloat16)
-    state_init = (
-        zero_rows,
-        zero_rows,
-        jnp.zeros((E, CG), jnp.float32),
-        saved_zero,
-        saved_zero,
-        saved_zero,
-    )
-    pieces = (
-        lax.all_gather(gate_proj, "dp", axis=0, tiled=True),
-        lax.all_gather(up_proj, "dp", axis=0, tiled=True),
-        lax.all_gather(down_proj, "dp", axis=0, tiled=True),
-    )
-    group = math.gcd(pieces[0].shape[0], 8)
-
-    def one(step, carry):
-        out_rows, grad_rows, slot_change, saved_active, saved_gate, saved_up = carry
-        first = step * group
-        tokens, rows, gate_here = expert_inputs(first, group)
-        upstream_rows = padded_grad[tokens].astype(jnp.float32)
-        w_gate = lax.dynamic_slice_in_dim(pieces[0], step * group, group, 0)
-        w_up = lax.dynamic_slice_in_dim(pieces[1], step * group, group, 0)
-        w_down = lax.dynamic_slice_in_dim(pieces[2], step * group, group, 0)
-        gate_pre = jnp.einsum("ecd,edf->ecf", rows, w_gate, preferred_element_type=jnp.float32)
-        up_pre = jnp.einsum("ecd,edf->ecf", rows, w_up, preferred_element_type=jnp.float32)
-        squash = jax.nn.sigmoid(gate_pre)
-        swish = gate_pre * squash
-        active = (swish * up_pre).astype(jnp.bfloat16)
-        result = jnp.einsum("ecf,edf->ecd", active, w_down, preferred_element_type=jnp.float32)
-        flat_tokens = tokens.reshape(-1)
-        out_rows = out_rows.at[flat_tokens].add((result * gate_here[..., None]).reshape(-1, D))
-        slot_change = lax.dynamic_update_slice_in_dim(
-            slot_change, jnp.sum(result * upstream_rows, -1), first, 0
-        )
-        grad_out = (upstream_rows * gate_here[..., None]).astype(jnp.bfloat16)
-        grad_active = jnp.einsum(
-            "ecd,edf->ecf", grad_out, w_down, preferred_element_type=jnp.float32
-        )
-        grad_gate = (grad_active * up_pre * squash * (1.0 + gate_pre * (1.0 - squash))).astype(
-            jnp.bfloat16
-        )
-        grad_up = (grad_active * swish).astype(jnp.bfloat16)
-        back_rows = jnp.einsum(
-            "ecf,edf->ecd", grad_gate, w_gate, preferred_element_type=jnp.float32
-        )
-        back_rows = back_rows + jnp.einsum(
-            "ecf,edf->ecd", grad_up, w_up, preferred_element_type=jnp.float32
-        )
-        grad_rows = grad_rows.at[flat_tokens].add(back_rows.reshape(-1, D))
-        saved_active = lax.dynamic_update_slice_in_dim(saved_active, active, first, 0)
-        saved_gate = lax.dynamic_update_slice_in_dim(saved_gate, grad_gate, first, 0)
-        saved_up = lax.dynamic_update_slice_in_dim(saved_up, grad_up, first, 0)
-        return (out_rows, grad_rows, slot_change, saved_active, saved_gate, saved_up)
-
-    state = lax.fori_loop(0, pieces[0].shape[0] // group, one, state_init)
-    moe_term, grad_rows, slot_change, saved_active, saved_gate, saved_up = state
-    (moe_local,) = sum_tokens((moe_term[:seq_len],))
+    all_post = lax.all_gather(post_normed, ("dp", "tensor"), axis=0, tiled=True)
+    rows = dispatch(plan, route, all_post, all_grad, router_full)
+    results, gate_weight_grad, up_weight_grad, down_weight_grad = experts(
+        plan, route, base, rows[0], gate_proj, up_proj, down_proj
+    )
+    moe_term, grad_term, router_part = combine(
+        plan, route, results, rows[1], all_post, router_full
+    )
+    moe_local = sum_all(moe_term)
+    grad_post = sum_all(grad_term)
+    router_part = router_part.T
     layer_out = (middle + moe_local).astype(jnp.bfloat16)[None]
-    slot_rows = padded_post[slot_token]
-    slot_out = (padded_grad[slot_token].astype(jnp.float32) * slot_gate[..., None]).astype(
-        jnp.bfloat16
-    )
-    owned_rows, owned_out, owned_gate, owned_up, owned_active = (
-        lax.all_to_all(slot_rows, "dp", split_axis=0, concat_axis=1, tiled=True),
-        lax.all_to_all(slot_out, "dp", split_axis=0, concat_axis=1, tiled=True),
-        lax.all_to_all(saved_gate, "dp", split_axis=0, concat_axis=1, tiled=True),
-        lax.all_to_all(saved_up, "dp", split_axis=0, concat_axis=1, tiled=True),
-        lax.all_to_all(saved_active, "dp", split_axis=0, concat_axis=1, tiled=True),
-    )
-    gate_weight_grad = jnp.einsum(
-        "ecd,ecf->edf", owned_rows, owned_gate, preferred_element_type=jnp.float32
-    )
-    up_weight_grad = jnp.einsum(
-        "ecd,ecf->edf", owned_rows, owned_up, preferred_element_type=jnp.float32
-    )
-    down_weight_grad = jnp.einsum(
-        "ecd,ecf->edf", owned_out, owned_active, preferred_element_type=jnp.float32
-    )
-    route_change = slot_change.reshape(-1)[slot].reshape(seq_len, TOP)
-    grad_post, gate_change = sum_tokens((grad_rows[:seq_len], route_change))
-    own_share = lax.dynamic_slice_in_dim(router_share, rank * shard, shard, 0)
-    own_choose = lax.dynamic_slice_in_dim(choose, rank * shard, shard, 0)
-    grad_share = jnp.sum(jnp.where(own_choose, gate_change[:, :, None], 0.0), 1)
-    grad_logits = own_share * (grad_share - jnp.sum(grad_share * own_share, -1, keepdims=True))
-    router_part = lax.dot_general(
-        post_normed.astype(jnp.float32),
-        grad_logits,
-        (((0,), (0,)), ((), ())),
-        precision=lax.Precision.HIGHEST,
-    )
-    grad_post = grad_post + lax.dot_general(
-        grad_logits,
-        router_full.astype(jnp.float32),
-        (((1,), (1,)), ((), ())),
-        precision=lax.Precision.HIGHEST,
-    )
     post_gain_part = jnp.sum(grad_post * middle * inv_post, 0)
     grad_middle = upstream.astype(jnp.float32) + norm_back(
         grad_post, middle, inv_post, post_gain, D
@@ -373,7 +682,7 @@
     normed_term = normed_term + lax.dot_general(
         grad_value, w_value, (((1,), (1,)), ((), ())), preferred_element_type=jnp.float32
     )
-    (grad_normed,) = sum_tokens((normed_term,))
+    grad_normed = sum_tokens(normed_term)
     pre_gain_part = jnp.sum(grad_normed * residual * inv_pre, 0)
     input_grad = (grad_middle + norm_back(grad_normed, residual, inv_pre, pre_gain, D)).astype(
         jnp.bfloat16

time: 4410 us -> 2310 us (0.52)
  local copies, waits for them, and re-layouts: 716 us -> 30.5 us
  waiting for transfers between devices: 2050 us -> 1380 us
  matrix products: 704 us -> 116 us
  other arithmetic: 581 us -> 69.2 us
  Pallas kernels: 0 us -> 463 us
  blocking collectives: 286 us -> 226 us
    all_gather x3 -> x2, waiting for transfers between devices: 1280 us -> 250 us  [the longest x1 197 us: body(): all_post = lax.all_gather(post_normed, ('dp', 'tensor'), axis=0, tiled=True)]
    dot_general x54 -> x1, matrix products: 598 us -> 0.24 us  [routing(): jnp.einsum('ts,bse->bte', earlier, ones, preferred_element_type=jnp.float32)]
    gather x19 -> x0, local copies, waits for them, and re-layouts: 481 us -> none  [the longest x8 123 us: one(): upstream_rows = padded_grad[tokens].astype(jnp.float32)]
    pallas_call x0 -> x3, Pallas kernels: none -> 463 us  [the longest x1 171 us: experts(): pl.pallas_call(expert_kernel, grid_spec=pltpu.PrefetchScalarGridSpec(num_...]
    scatter-add x16 -> x0, other arithmetic: 442 us -> none  [the longest x8 221 us: one(): out_rows.at[flat_tokens].add((result * gate_here[..., None]).reshape(-1, D))]
    all_to_all x4 -> x0, waiting for transfers between devices: 211 us -> none  [the longest x1 205 us: body(): lax.all_to_all(slot_out, 'dp', split_axis=0, concat_axis=1, tiled=True)]
    reduce_scatter x6, waiting for transfers between devices: 382 us -> 587 us  [the longest x2 305 us: sum_all(): lax.psum_scatter(part, 'dp', scatter_dimension=0, tiled=True)]
    unnamed x25 -> x24, waiting for transfers between devices: 4.87 us -> 204 us
  transfers between devices with their start and end apart: 27 -> 21, of which waited for: 14 -> 19; matrix products, arithmetic and copies ran while one was open for 45% -> 8% of each run, Pallas kernels for 0% -> 0%
where the time goes in v1:
time: 2310 us; the launch traced here: 2300 us
  waiting for transfers between devices  1380 us (60%)
  Pallas kernels  463 us (20%)
  blocking collectives  226 us (10%)
  matrix products  116 us (5%)
  other arithmetic  69.2 us (3%)
  local copies, waits for them, and re-layouts  30.5 us (1%)
    reduce_scatter x2, waiting for transfers between devices, sum_all(): lax.psum_scatter(part, 'dp', scatter_dimension=0, tiled=True)  305 us
    reduce_scatter x4, waiting for transfers between devices, sum_tokens(): lax.psum_scatter(part.astype(jnp.bfloat16), 'tensor', scatter_dimension=0...  282 us
    unnamed x24, waiting for transfers between devices  204 us
    all_gather x1, waiting for transfers between devices, body(): all_post = lax.all_gather(post_normed, ('dp', 'tensor'), axis=0, tiled=True)  197 us
    pallas_call x1, Pallas kernels, experts(): pl.pallas_call(expert_kernel, grid_spec=pltpu.PrefetchScalarGridSpec(num_...  171 us
    pallas_call x1, Pallas kernels, dispatch(): pl.pallas_call(dispatch_kernel, grid_spec=pltpu.PrefetchScalarGridSpec(nu...  157 us
    all_gather x2, waiting for transfers between devices, gather_tokens(): lax.all_gather(as_sent(parts), 'tensor', axis=0, tiled=True)  137 us
    pallas_call x1, Pallas kernels, combine(): pl.pallas_call(combine_kernel, grid_spec=pltpu.PrefetchScalarGridSpec(num...  135 us
  transfers between devices with their start and end apart: 21, of which 19 were waited for; matrix products, arithmetic and copies ran while one was open for 8% of the time, Pallas kernels for 0%

profile of v1, /device:TPU:0, one launch (start us, length us, event | category | flops | bytes accessed | tf_op | source)
XLA Modules:
  0.0 2301.0 jit_solution(10906991220731784600)
XLA Ops:
  10.5 42.0 %all-reduce.7 = (bf16[2048]{0:T(1024)(128)(2,1)S(1)}, bf16[2048]{0:T(1024)(128)(2,1)S(1)}) all-reduce(bf16[2048]{0:T(1024)(128)(2,1)S(1)} %dynamic-update-slice, bf16[2048]{0:T(1024)(128)(2,1)S(1)} %dynamic-update-slice.1), channel_id=1, replica_groups=mesh['dp'=8,'tensor'=4] {'dp','tensor'}, use_global_device_ids=true, to_apply=%add | all-reduce | flops 4096 | bytes 16384
  80.4 57.0 %all-gather.13.cloned.1.call-done = bf16[1024,2048]{1,0:T(8,128)(2,1)} async-done(((bf16[256,2048]{1,0:T(8,128)(2,1)}), bf16[1024,2048]{1,0:T(8,128)(2,1)}) %all-gather.13.cloned.1.call-update) | async-done | bytes 4194320 | tf_op jit(solution)/shard_map/all_gather | solution.py:45
  142.7 23.1 %all-gather.17.cloned.1.call-done = bf16[2048,512]{1,0:T(8,128)(2,1)} async-done(((bf16[256,512]{1,0:T(8,128)(2,1)}), bf16[2048,512]{1,0:T(8,128)(2,1)}) %all-gather.17.cloned.1.call-update) | async-done | bytes 2097168 | tf_op jit(solution)/shard_map/all_gather | solution.py:571
  231.8 92.0 %reduce-scatter.20.cloned.1.call-done = bf16[256,2048]{1,0:T(8,128)(2,1)} async-done(((bf16[1024,2048]{1,0:T(8,128)(2,1)}), bf16[256,2048]{1,0:T(8,128)(2,1)}) %reduce-scatter.20.cloned.1.call-update) | async-done | bytes 1048592 | tf_op jit(solution)/shard_map/reduce_scatter | solution.py:51
  347.4 93.6 %all_gather.54.router.refs_35_ = bf16[2048,64]{1,0:T(8,128)(2,1)} all-gather(bf16[64,64]{1,0:T(8,128)(2,1)S(1)} %copy-done.53), channel_id=1, replica_groups=mesh['dp'=8,'tensor'=4] {'dp','tensor'}, dimensions={0}, use_global_device_ids=true | all-gather | bytes 270336 | tf_op jit(solution)/shard_map/all_gather | solution.py:564
  442.7 52.6 %all-gather.27.cloned.1.call-done = bf16[1,8192,2048]{2,1,0:T(8,128)(2,1)} async-done(((bf16[1,256,2048]{2,1,0:T(8,128)(2,1)}), bf16[1,8192,2048]{2,1,0:T(8,128)(2,1)}) %all-gather.27.cloned.1.call-update) | async-done | bytes 33554448 | tf_op jit(solution)/shard_map/all_gather | solution.py:587
  495.3 197.5 %all-gather.23.cloned.1.call-done.post.refs_34_ = bf16[8192,2048]{1,0:T(8,128)(2,1)} async-done(((bf16[256,2048]{1,0:T(8,128)(2,1)}), bf16[8192,2048]{1,0:T(8,128)(2,1)}) %all-gather.23.cloned.1.call-update) | async-done | bytes 33554448 | tf_op jit(solution)/shard_map/all_gather | solution.py:613
  692.8 156.8 %dispatch.1 = (bf16[24320,4224]{1,0:T(8,128)(2,1)}, bf16[8192,128]{1,0:T(8,128)(2,1)}) custom-call(s32[1]{0:T(128)} %bitcast.28.used, s32[95]{0:T(128)} %copy-done.71, s32[95]{0:T(128)} %fusion.66.part, bf16[8192,2048]{1,0:T(8,128)(2,1)} %all-gather.23.cloned.1.call-done.post.refs_34_, bf16[8192,2048]{1,0:T(8,128)(2,1)} %bitcast.251, ...), custom_call_target="tpu_custom_call" | custom-call | flops 52596572160 | bytes 410910720 | tf_op jit(solution)/shard_map/dispatch/pallas_call | solution.py:276
  849.6 170.9 %experts.1 = (bf16[16384,4224]{1,0:T(8,128)(2,1)}, f32[8,2048,256]{2,1,0:T(8,128)}, f32[8,2048,256]{2,1,0:T(8,128)}, f32[8,2048,256]{2,1,0:T(8,128)}) custom-call(s32[1024]{0:T(1024)} %bitcast.244, s32[8]{0:T(128)} %get-tuple-element.235.tiles, s32[8]{0:T(128)} %get-tuple-element.234.filled, s32[1]{0:T(128)} %bitcast.27.base, ...), custom_call_target="tpu_custom_call" | custom-call | flops 96636764160 | bytes 173015040 | tf_op jit(solution)/shard_map/experts/pallas_call | solution.py:390
  1020.5 135.3 %combine.1 = (bf16[8192,2048]{1,0:T(8,128)(2,1)}, bf16[8192,2048]{1,0:T(8,128)(2,1)}, f32[64,2048]{1,0:T(8,128)}) custom-call(s32[1]{0:T(128)} %bitcast.20.joined, s32[63]{0:T(128)} %copy-done.56, s32[63]{0:T(128)} %copy-done.61, s32[63]{0:T(128)} %compare_convert_fusion.last, s32[2016]{0:T(1024)} %reshape.553.target, ...), custom_call_target="tpu_custom_call" | custom-call | flops 69759664128 | bytes 138412032 | tf_op jit(solution)/shard_map/combine/pallas_call | solution.py:490
  1155.8 218.6 %reduce-scatter.26.cloned.1.call-done = bf16[1024,2048]{1,0:T(8,128)(2,1)} async-done(((bf16[8192,2048]{1,0:T(8,128)(2,1)}), bf16[1024,2048]{1,0:T(8,128)(2,1)}) %reduce-scatter.26.cloned.1.call-update) | async-done | bytes 4194320 | tf_op jit(solution)/shard_map/reduce_scatter | solution.py:57
  1374.5 79.0 %reduce-scatter.28.cloned.1.call-done = bf16[256,2048]{1,0:T(8,128)(2,1)} async-done(((bf16[1024,2048]{1,0:T(8,128)(2,1)}), bf16[256,2048]{1,0:T(8,128)(2,1)}) %reduce-scatter.28.cloned.1.call-update) | async-done | bytes 1048592 | tf_op jit(solution)/shard_map/reduce_scatter | solution.py:51
  1459.7 79.9 %all-gather.25.cloned.1.call-done = bf16[1024,2048]{1,0:T(8,128)(2,1)} async-done(((bf16[256,2048]{1,0:T(8,128)(2,1)}), bf16[1024,2048]{1,0:T(8,128)(2,1)}) %all-gather.25.cloned.1.call-update) | async-done | bytes 4194320 | tf_op jit(solution)/shard_map/all_gather | solution.py:45
  1661.1 86.1 %reduce-scatter.22.cloned.1.call-done = bf16[1024,2048]{1,0:T(8,128)(2,1)} async-done(((bf16[8192,2048]{1,0:T(8,128)(2,1)}), bf16[1024,2048]{1,0:T(8,128)(2,1)}) %reduce-scatter.22.cloned.1.call-update) | async-done | bytes 4194320 | tf_op jit(solution)/shard_map/reduce_scatter | solution.py:57
  1749.7 32.5 %reduce-scatter.40.cloned.1.call-done = bf16[16,4]{1,0:T(8,128)(2,1)} async-done(((bf16[128,4]{1,0:T(8,128)(2,1)}), bf16[16,4]{1,0:T(8,128)(2,1)}) %reduce-scatter.40.cloned.1.call-update) | async-done | bytes 144
  1783.5 33.6 %reduce-scatter.42.cloned.1.call-done = bf16[16,4]{1,0:T(8,128)(2,1)} async-done(((bf16[128,4]{1,0:T(8,128)(2,1)}), bf16[16,4]{1,0:T(8,128)(2,1)}) %reduce-scatter.42.cloned.1.call-update) | async-done | bytes 144
  1818.5 43.2 %reduce-scatter.32.cloned.1.call-done = bf16[256,512]{1,0:T(8,128)(2,1)} async-done(((bf16[2048,512]{1,0:T(8,128)(2,1)}), bf16[256,512]{1,0:T(8,128)(2,1)}) %reduce-scatter.32.cloned.1.call-update) | async-done | bytes 262160 | tf_op jit(solution)/shard_map/reduce_scatter | solution.py:691
  1863.5 42.9 %reduce-scatter.34.cloned.1.call-done = bf16[256,512]{1,0:T(8,128)(2,1)} async-done(((bf16[2048,512]{1,0:T(8,128)(2,1)}), bf16[256,512]{1,0:T(8,128)(2,1)}) %reduce-scatter.34.cloned.1.call-update) | async-done | bytes 262160 | tf_op jit(solution)/shard_map/reduce_scatter | solution.py:694
  1908.2 42.6 %reduce-scatter.36.cloned.1.call-done = bf16[256,512]{1,0:T(8,128)(2,1)} async-done(((bf16[2048,512]{1,0:T(8,128)(2,1)}), bf16[256,512]{1,0:T(8,128)(2,1)}) %reduce-scatter.36.cloned.1.call-update) | async-done | bytes 262160 | tf_op jit(solution)/shard_map/reduce_scatter | solution.py:697
  1952.6 43.0 %reduce-scatter.38.cloned.1.call-done = bf16[256,512]{1,0:T(8,128)(2,1)} async-done(((bf16[2048,512]{1,0:T(8,128)(2,1)}), bf16[256,512]{1,0:T(8,128)(2,1)}) %reduce-scatter.38.cloned.1.call-update) | async-done | bytes 262160 | tf_op jit(solution)/shard_map/reduce_scatter | solution.py:700
  1997.4 77.1 %reduce-scatter.30.cloned.1.call-done = bf16[256,2048]{1,0:T(8,128)(2,1)} async-done(((bf16[1024,2048]{1,0:T(8,128)(2,1)}), bf16[256,2048]{1,0:T(8,128)(2,1)}) %reduce-scatter.30.cloned.1.call-update) | async-done | bytes 1048592 | tf_op jit(solution)/shard_map/reduce_scatter | solution.py:51
  2076.4 43.2 %all-reduce.4 = (f32[2048]{0:T(1024)S(1)}, f32[2048]{0:T(1024)S(1)}) all-reduce(f32[2048]{0:T(1024)S(1)} %get-tuple-element.173, f32[2048]{0:T(1024)S(1)} %copy-done.46), channel_id=10, replica_groups=mesh['dp'=8,'tensor'=4] {'dp','tensor'}, use_global_device_ids=true, to_apply=%region_42.43.clone | all-reduce | flops 4096 | bytes 32768
  2120.7 34.4 %reduce-scatter.24.cloned.1.call-done = bf16[256,2048]{1,0:T(8,128)(2,1)} async-done(((bf16[1024,2048]{1,0:T(8,128)(2,1)}), bf16[256,2048]{1,0:T(8,128)(2,1)}) %reduce-scatter.24.cloned.1.call-update) | async-done | bytes 1048592 | tf_op jit(solution)/shard_map/reduce_scatter | solution.py:51
  2159.5 134.3 %reduce-scatter.44.cloned.1.call-done = f32[64,64]{1,0:T(8,128)} async-done(((f32[2048,64]{1,0:T(8,128)}), f32[64,64]{1,0:T(8,128)}) %reduce-scatter.44.cloned.1.call-update) | async-done | bytes 16400
  (323 shorter events, 272.3 us)
Async XLA Ops:
  8.0 72.4 %all-gather.19.cloned.1.call-start = ((), (), s32[]{:S(2)}) async-start(), calls=%async_computation.16 | async-start | bytes 2359296 | tf_op jit(solution)/shard_map/all_gather | solution.py:572
  8.8 128.6 %all-gather.13.cloned.1.call-start = ((), (), s32[]{:S(2)}) async-start(), calls=%async_computation.13 | async-start | bytes 5242880 | tf_op jit(solution)/shard_map/all_gather | solution.py:45
  56.5 109.2 %all-gather.17.cloned.1.call-start = ((), (), s32[]{:S(2)}) async-start(), calls=%async_computation.15 | async-start | bytes 2359296 | tf_op jit(solution)/shard_map/all_gather | solution.py:571
  57.3 141.8 %all-gather.15.cloned.1.call-start = ((), (), s32[]{:S(2)}) async-start(), calls=%async_computation.14 | async-start | bytes 2359296 | tf_op jit(solution)/shard_map/all_gather | solution.py:573
  57.8 167.2 %all-gather.21.cloned.1.call-start = ((), (), s32[]{:S(2)}) async-start(), calls=%async_computation.17 | async-start | bytes 2359296 | tf_op jit(solution)/shard_map/all_gather | solution.py:574
  58.4 265.3 %reduce-scatter.20.cloned.1.call-start = ((), (), s32[]{:S(2)}) async-start(), calls=%async_computation.18 | async-start | bytes 5242880 | tf_op jit(solution)/shard_map/reduce_scatter | solution.py:51
  231.1 264.2 %all-gather.27.cloned.1.call-start = ((), (), s32[]{:S(2)}) async-start(), calls=%async_computation.30 | async-start | bytes 34603008 | tf_op jit(solution)/shard_map/all_gather | solution.py:587
  231.7 461.1 %all-gather.23.cloned.1.call-start = ((), (), s32[]{:S(2)}) async-start(), calls=%async_computation.19 | async-start | bytes 34603008 | tf_op jit(solution)/shard_map/all_gather | solution.py:613
  328.1 1046.4 %reduce-scatter.26.cloned.1.call-start = ((), (), s32[]{:S(2)}) async-start(), calls=%async_computation.22 | async-start | bytes 37748736 | tf_op jit(solution)/shard_map/reduce_scatter | solution.py:57
  346.6 346.2 %copy-start.71 = (s32[95]{0:T(128)}, s32[95]{0:T(128)S(1)}, u32[]{:S(2)}) copy-start(s32[95]{0:T(128)S(1)} %broadcast_add_fusion.1.block) | copy-start | bytes 1144
  1155.8 297.8 %reduce-scatter.28.cloned.1.call-start = ((), (), s32[]{:S(2)}) async-start(), calls=%async_computation.23 | async-start | bytes 5242880 | tf_op jit(solution)/shard_map/reduce_scatter | solution.py:51
  1374.5 165.1 %all-gather.25.cloned.1.call-start = ((), (), s32[]{:S(2)}) async-start(), calls=%async_computation.24 | async-start | bytes 5242880 | tf_op jit(solution)/shard_map/all_gather | solution.py:45
  1458.2 289.1 %reduce-scatter.22.cloned.1.call-start = ((), (), s32[]{:S(2)}) async-start(), calls=%async_computation.20 | async-start | bytes 37748736 | tf_op jit(solution)/shard_map/reduce_scatter | solution.py:57
  1458.8 323.4 %reduce-scatter.40.cloned.1.call-start = ((), (), s32[]{:S(2)}) async-start(), calls=%async_computation.31 | async-start | bytes 36864
  1605.5 211.6 %reduce-scatter.42.cloned.1.call-start = ((), (), s32[]{:S(2)}) async-start(), calls=%async_computation.32 | async-start | bytes 36864
  1610.3 251.4 %reduce-scatter.32.cloned.1.call-start = ((), (), s32[]{:S(2)}) async-start(), calls=%async_computation.26 | async-start | bytes 2359296 | tf_op jit(solution)/shard_map/reduce_scatter | solution.py:691
  1617.3 289.1 %reduce-scatter.34.cloned.1.call-start = ((), (), s32[]{:S(2)}) async-start(), calls=%async_computation.27 | async-start | bytes 2359296 | tf_op jit(solution)/shard_map/reduce_scatter | solution.py:694
  1625.2 325.6 %reduce-scatter.36.cloned.1.call-start = ((), (), s32[]{:S(2)}) async-start(), calls=%async_computation.28 | async-start | bytes 2359296 | tf_op jit(solution)/shard_map/reduce_scatter | solution.py:697
  1639.7 355.9 %reduce-scatter.38.cloned.1.call-start = ((), (), s32[]{:S(2)}) async-start(), calls=%async_computation.29 | async-start | bytes 2359296 | tf_op jit(solution)/shard_map/reduce_scatter | solution.py:700
  1647.1 427.4 %reduce-scatter.30.cloned.1.call-start = ((), (), s32[]{:S(2)}) async-start(), calls=%async_computation.25 | async-start | bytes 5242880 | tf_op jit(solution)/shard_map/reduce_scatter | solution.py:51
  1661.1 494.0 %reduce-scatter.24.cloned.1.call-start = ((), (), s32[]{:S(2)}) async-start(), calls=%async_computation.21 | async-start | bytes 5242880 | tf_op jit(solution)/shard_map/reduce_scatter | solution.py:51
  1747.3 546.5 %reduce-scatter.44.cloned.1.call-start = ((), (), s32[]{:S(2)}) async-start(), calls=%async_computation.33 | async-start | bytes 1081344
  1749.7 324.8 %copy-start.35 = (f32[2048]{0:T(1024)S(1)}, f32[2048]{0:T(1024)}, u32[]{:S(2)}) copy-start(f32[2048]{0:T(1024)} %copy-done.34) | copy-start | bytes 24580
  1749.7 324.8 %copy-start.51 = (f32[256]{0:T(256)S(1)}, f32[256]{0:T(256)}, u32[]{:S(2)}) copy-start(f32[256]{0:T(256)} %copy-done.50) | copy-start | bytes 3076
  (73 other events, 3007.5 us)
Sparse Core Ops, SparseCore 0:
  10.7 30.7 all-gather.18
  56.6 80.6 all-gather.12
  139.3 26.4 all-gather.16
  167.5 27.8 all-gather.14
  197.1 27.8 all-gather.20
  231.2 92.4 reduce-scatter.19
  1155.9 218.4 reduce-scatter.25
  1376.7 76.7 reduce-scatter.27
  1458.3 81.2 all-gather.24
  1543.4 203.7 reduce-scatter.21
  1750.8 31.2 reduce-scatter.39
  1785.9 31.2 reduce-scatter.41
  1820.4 41.1 reduce-scatter.31
  1865.1 41.2 reduce-scatter.33
  1909.5 41.2 reduce-scatter.35
  1954.3 41.2 reduce-scatter.37
  1997.7 76.7 reduce-scatter.29
  2076.7 78.3 reduce-scatter.23
  2157.9 135.7 reduce-scatter.43
Sparse Core Ops, SparseCore 1:
  234.9 260.3 all-gather.26
  499.1 193.6 all-gather.22

commit v2 on v1

--- a/solution.py
+++ b/solution.py
@@ -18,10 +18,6 @@
 masked_score = -1000000000.0
 
 
-def as_sent(value):
-    return jax.tree.map(lambda a: a.astype(jnp.bfloat16) if a.dtype == jnp.float32 else a, value)
-
-
 def rope_tables(length, width):
     positions = jnp.arange(length).astype(jnp.float32)
     rates = 10000.0 ** (-jnp.arange(0, width, 2).astype(jnp.float32) / width)
@@ -37,24 +33,6 @@
 def rotate_back(tensor):
     half = tensor.shape[-1] // 2
     return jnp.concatenate([tensor[..., half:], -tensor[..., :half]], -1)
-
-
-def gather_tokens(parts):
-    return jax.tree.map(
-        lambda part, own: part.astype(own.dtype),
-        lax.all_gather(as_sent(parts), "tensor", axis=0, tiled=True),
-        parts,
-    )
-
-
-def sum_tokens(part):
-    return lax.psum_scatter(
-        part.astype(jnp.bfloat16), "tensor", scatter_dimension=0, tiled=True
-    ).astype(jnp.float32)
-
-
-def sum_all(part):
-    return sum_tokens(lax.psum_scatter(part, "dp", scatter_dimension=0, tiled=True))
 
 
 def sum_heads(parts):
@@ -125,14 +103,632 @@
     return (grad_query.reshape(query.shape), jnp.sum(grad_keys, 0), jnp.sum(grad_values, 0))
 
 
+MESH = pl.DeviceIdType.MESH
+VMEM = 60 * 1024 * 1024
+
+
+def transfer(microseconds):
+    return pl.CostEstimate(flops=0, bytes_accessed=microseconds * 3_000_000, transcendentals=0)
+
+
+def flip(index, bit):
+    return index + bit - 2 * bit * ((index // bit) % 2)
+
+
+def send(source, target, send_sem, recv_sem, device):
+    return pltpu.make_async_remote_copy(
+        src_ref=source,
+        dst_ref=target,
+        send_sem=send_sem,
+        recv_sem=recv_sem,
+        device_id=device,
+        device_id_type=MESH,
+    )
+
+
+def greet(devices, extra=()):
+    barrier = pltpu.get_barrier_semaphore()
+    for device in devices:
+        pl.semaphore_signal(barrier, inc=1, device_id=device, device_id_type=MESH)
+    for there, device in extra:
+
+        @pl.when(there)
+        def _(device=device):
+            pl.semaphore_signal(barrier, inc=1, device_id=device, device_id_type=MESH)
+
+    count = len(devices)
+    for there, _ in extra:
+        count = count + jnp.where(there, 1, 0)
+    pl.semaphore_wait(barrier, count)
+
+
+def both_ways(n):
+    spot = lax.axis_index("tensor")
+    return spot, (
+        (spot < n - 1, {"tensor": jnp.minimum(spot + 1, n - 1)}),
+        (spot > 0, {"tensor": jnp.maximum(spot - 1, 0)}),
+    )
+
+
+def shard_at(spot, way, distance, n):
+    number = spot - distance if way == 0 else spot + distance
+    return (number >= 0) & (number < n), jnp.clip(number, 0, n - 1)
+
+
+def chain_gather_kernel(n, pieces, own, _later, out, _passed, local_sem, send_sem, recv_sem):
+    spot, sides = both_ways(n)
+    rows = own.shape[0] // pieces
+    greet([], sides)
+    keep = pltpu.make_async_copy(own, out.at[spot], local_sem)
+    keep.start()
+
+    def copy(way, distance, piece):
+        there, number = shard_at(spot, way, distance, n)
+        part = pl.ds(piece * rows, rows)
+        source = own.at[part] if distance == 0 else out.at[number, part]
+        return there & sides[way][0], send(
+            source,
+            out.at[number, part],
+            send_sem.at[way, distance, piece],
+            recv_sem.at[way, distance, piece],
+            sides[way][1],
+        )
+
+    def arrived(way, distance, piece):
+        there, number = shard_at(spot, way, distance, n)
+        part = pl.ds(piece * rows, rows)
+
+        @pl.when(there)
+        def _():
+            send(
+                out.at[number, part],
+                out.at[number, part],
+                send_sem.at[way, distance - 1, piece],
+                recv_sem.at[way, distance - 1, piece],
+                sides[way][1],
+            ).wait_recv()
+
+    for distance in range(n):
+        for piece in range(pieces):
+            for way in (0, 1):
+                if distance:
+                    arrived(way, distance, piece)
+                if distance < n - 1:
+                    go, one = copy(way, distance, piece)
+
+                    @pl.when(go)
+                    def _(one=one):
+                        one.start()
+
+    keep.wait()
+    for distance in range(n - 1):
+        for piece in range(pieces):
+            for way in (0, 1):
+                go, one = copy(way, distance, piece)
+
+                @pl.when(go)
+                def _(one=one):
+                    one.wait_send()
+
+
+def chain_gather(own, later, number, pieces=4):
+    n = lax.axis_size("tensor")
+    rows, width = own.shape
+    anywhere = pl.BlockSpec(memory_space=pl.ANY)
+    out, later = pl.pallas_call(
+        functools.partial(chain_gather_kernel, n, pieces),
+        out_shape=[
+            jax.ShapeDtypeStruct((n, rows, width), own.dtype),
+            jax.ShapeDtypeStruct(later.shape, later.dtype),
+        ],
+        in_specs=[anywhere] * 2,
+        out_specs=[anywhere] * 2,
+        input_output_aliases={1: 1},
+        scratch_shapes=[
+            pltpu.SemaphoreType.DMA,
+            pltpu.SemaphoreType.DMA((2, n - 1, pieces)),
+            pltpu.SemaphoreType.DMA((2, n - 1, pieces)),
+        ],
+        compiler_params=pltpu.CompilerParams(collective_id=number, has_side_effects=True),
+        cost_estimate=transfer(65),
+        name="chain_gather",
+    )(own, later)
+    return out.reshape(n * rows, width), later
+
+
+def add_into(target, source, rows, start=0, source_start=0):
+    step = 16
+
+    def body(index, carry):
+        at = pl.ds(pl.multiple_of(start + index * step, step), step)
+        come = pl.ds(pl.multiple_of(source_start + index * step, step), step)
+        target[at, :] = (
+            target[at, :].astype(jnp.float32) + source[come, :].astype(jnp.float32)
+        ).astype(target.dtype)
+        return carry
+
+    lax.fori_loop(0, rows // step, body, 0)
+
+
+def chain_sum_kernel(n, pieces, part, _later, out, _passed, held, send_sem, recv_sem):
+    spot, sides = both_ways(n)
+    rows = out.shape[0] // pieces
+    greet([], sides)
+
+    def copy(way, far, piece, mine):
+        number = spot + far if way == 0 else spot - far
+        there = (number >= 0) & (number < n)
+        number = jnp.clip(number, 0, n - 1)
+        at = pl.ds(piece * rows, rows)
+        source = part.at[number, at]
+        return there, number, send(
+            source if mine else held.at[way, far, at],
+            held.at[way, far - 1, at],
+            send_sem.at[way, far - 1, piece],
+            recv_sem.at[way, far - 1, piece],
+            sides[way][1],
+        )
+
+    def arrived(way, far, piece):
+        at = pl.ds(piece * rows, rows)
+        send(
+            held.at[way, far, at],
+            held.at[way, far, at],
+            send_sem.at[way, far, piece],
+            recv_sem.at[way, far, piece],
+            sides[way][1],
+        ).wait_recv()
+
+    for far in range(n - 1, 0, -1):
+        for piece in range(pieces):
+            for way in (0, 1):
+                behind = sides[1 - way][0]
+                there, number, first = copy(way, far, piece, True)
+
+                @pl.when(there & jnp.logical_not(behind))
+                def _(first=first):
+                    first.start()
+
+                if far < n - 1:
+                    _, _, onward = copy(way, far, piece, False)
+
+                    @pl.when(there & behind)
+                    def _(way=way, far=far, piece=piece, number=number, onward=onward):
+                        arrived(way, far, piece)
+                        add_into(
+                            held.at[way, far], part.at[number], rows, piece * rows, piece * rows
+                        )
+                        onward.start()
+
+    for piece in range(pieces):
+        at = pl.ds(piece * rows, rows)
+
+        def body(index, carry):
+            here = pl.ds(pl.multiple_of(piece * rows + index * 16, 16), 16)
+            out[here, :] = part[spot, here, :].astype(jnp.float32)
+            return carry
+
+        lax.fori_loop(0, rows // 16, body, 0)
+        for way in (0, 1):
+
+            @pl.when(sides[1 - way][0])
+            def _(way=way):
+                arrived(way, 0, piece)
+                add_into(out, held.at[way, 0], rows, piece * rows, piece * rows)
+
+    for far in range(n - 1, 0, -1):
+        for piece in range(pieces):
+            for way in (0, 1):
+                there, _, one = copy(way, far, piece, True)
+
+                @pl.when(there)
+                def _(one=one):
+                    one.wait_send()
+
+
+def chain_sum(part, later, number, pieces=4):
+    n = lax.axis_size("tensor")
+    width = part.shape[1]
+    rows = part.shape[0] // n
+    anywhere = pl.BlockSpec(memory_space=pl.ANY)
+    inside = pl.BlockSpec(memory_space=pltpu.VMEM)
+    return pl.pallas_call(
+        functools.partial(chain_sum_kernel, n, pieces),
+        out_shape=[
+            jax.ShapeDtypeStruct((rows, width), jnp.float32),
+            jax.ShapeDtypeStruct(later.shape, later.dtype),
+        ],
+        in_specs=[inside, anywhere],
+        out_specs=[inside, anywhere],
+        input_output_aliases={1: 1},
+        scratch_shapes=[
+            pltpu.VMEM((2, n - 1, rows, width), part.dtype),
+            pltpu.SemaphoreType.DMA((2, n - 1, pieces)),
+            pltpu.SemaphoreType.DMA((2, n - 1, pieces)),
+        ],
+        compiler_params=pltpu.CompilerParams(
+            collective_id=number, has_side_effects=True, vmem_limit_bytes=VMEM
+        ),
+        cost_estimate=transfer(65),
+        name="chain_sum",
+    )(part.reshape(n, rows, width), later)
+
+
+def box_devices():
+    me = lax.axis_index("dp")
+    return me, {bit: {"dp": flip(me, bit)} for bit in (1, 2, 4)}
+
+
+def box_gather_kernel(n, own, out, local_sem, z_send, z_recv, near_send, near_recv, on_send, on_recv, side_send, side_recv):
+    spot, sides = both_ways(n)
+    me, near = box_devices()
+    half = own.shape[0] // 2
+    greet([near[1], near[2], near[4]], sides)
+    keep = pltpu.make_async_copy(own, out.at[me, spot], local_sem)
+    keep.start()
+    sends = []
+
+    def piece(seq, shard, part):
+        return out.at[seq, shard, pl.ds(part * half, half)]
+
+    def start(condition, one):
+        sends.append((condition, one))
+
+        @pl.when(condition)
+        def _():
+            one.start()
+
+    def await_piece(condition, target, recv):
+        @pl.when(condition)
+        def _():
+            send(target, target, side_send.at[0, 0, 0], recv, near[1]).wait_recv()
+
+    def to_side(condition, slot, seq, shard, part, source):
+        start(condition, send(source, piece(seq, shard, part), side_send.at[slot, shard, part], side_recv.at[slot, shard, part], near[1]))
+
+    def mine(way, distance):
+        there, shard = shard_at(spot, way, distance, n)
+        for part in (0, 1):
+            if distance:
+                await_piece(there, piece(me, shard, part), z_recv.at[way, distance - 1, part])
+            source = piece(me, shard, part) if distance else own.at[pl.ds(part * half, half)]
+            for out_way in (0, 1) if distance == 0 else (way,):
+                if distance < n - 1:
+                    start(there & sides[out_way][0], send(source, piece(me, shard, part), z_send.at[out_way, distance, part], z_recv.at[out_way, distance, part], sides[out_way][1]))
+            for axis, bit in ((0, 2), (1, 4)):
+                start(there, send(source, piece(me, shard, part), near_send.at[axis, shard, part], near_recv.at[axis, shard, part], near[bit]))
+            to_side(there, 0, me, shard, part, source)
+
+    def nearby(way, distance):
+        there, shard = shard_at(spot, way, distance, n)
+        for part in (0, 1):
+            for axis, bit in ((0, 2), (1, 4)):
+                seq = flip(me, bit)
+                source = piece(seq, shard, part)
+                await_piece(there, source, near_recv.at[axis, shard, part])
+                if part == axis:
+                    start(there, send(source, source, on_send.at[1 - axis, shard], on_recv.at[1 - axis, shard], near[6 - bit]))
+                to_side(there, 1 + axis, seq, shard, part, source)
+
+    def far(way, distance):
+        there, shard = shard_at(spot, way, distance, n)
+        seq = flip(flip(me, 2), 4)
+        for part in (0, 1):
+            source = piece(seq, shard, part)
+            await_piece(there, source, on_recv.at[1 - part, shard])
+            to_side(there, 3, seq, shard, part, source)
+
+    for step in range(n + 2):
+        for task, delay in ((mine, 0), (nearby, 1), (far, 2)):
+            distance = step - delay
+            if 0 <= distance < n:
+                for way in (0, 1) if distance else (0,):
+                    task(way, distance)
+    for shard in range(n):
+        for part in (0, 1):
+            for slot, bit in enumerate((0, 2, 4, 6)):
+                seq = flip(me, 1)
+                for one in (2, 4):
+                    if bit & one:
+                        seq = flip(seq, one)
+                await_piece(spot >= 0, piece(seq, shard, part), side_recv.at[slot, shard, part])
+    keep.wait()
+    for condition, one in sends:
+
+        @pl.when(condition)
+        def _(one=one):
+            one.wait_send()
+
+
+def box_gather(own):
+    n = lax.axis_size("tensor")
+    rows, width = own.shape
+    sem = pltpu.SemaphoreType.DMA
+    out = pl.pallas_call(
+        functools.partial(box_gather_kernel, n),
+        out_shape=jax.ShapeDtypeStruct((8, n, rows, width), own.dtype),
+        in_specs=[pl.BlockSpec(memory_space=pl.ANY)],
+        out_specs=pl.BlockSpec(memory_space=pl.ANY),
+        scratch_shapes=[sem]
+        + [sem((2, n - 1, 2))] * 2
+        + [sem((2, n, 2))] * 2
+        + [sem((2, n))] * 2
+        + [sem((4, n, 2))] * 2,
+        compiler_params=pltpu.CompilerParams(collective_id=3, has_side_effects=True),
+        cost_estimate=transfer(140),
+        name="box_gather",
+    )(own)
+    return out.reshape(8 * n * rows, width)
+
+
+def order_of(spot, n):
+    table = [sorted(range(n), key=lambda s: -abs(s - j)) for j in range(n)]
+    result = []
+    for step in range(n):
+        value = jnp.int32(table[0][step])
+        for j in range(1, n):
+            value = jnp.where(spot == j, table[j][step], value)
+        result.append(value)
+    return result
+
+
+def box_sum_kernel(n, part, _later, out, _passed, side, local, on, near, chain, local_sem, side_send, side_recv, on_send, on_recv, near_send, near_recv, z_send, z_recv):
+    spot, sides = both_ways(n)
+    me, close = box_devices()
+    half = out.shape[0] // 2
+    rows = out.shape[0]
+    greet([close[1], close[2], close[4]], sides)
+    order = order_of(spot, n)
+    bits = (6, 2, 4, 0)
+    sends = []
+
+    def seq_of(index, bit):
+        for one in (2, 4):
+            if bit & one:
+                index = flip(index, one)
+        return index
+
+    def start(one, condition=None):
+        sends.append((condition, one))
+        if condition is None:
+            one.start()
+        else:
+
+            @pl.when(condition)
+            def _():
+                one.start()
+
+    def await_at(target, recv):
+        send(target, target, side_send.at[0, 0], recv, close[1]).wait_recv()
+
+    def loads(chip, shard):
+        return pltpu.make_async_copy(part.at[seq_of(me, bits[chip]), shard], local.at[chip, shard], local_sem.at[chip, shard])
+
+    for shard in order:
+        for chip in range(4):
+            start(send(part.at[seq_of(flip(me, 1), bits[chip]), shard], side.at[chip, shard], side_send.at[chip, shard], side_recv.at[chip, shard], close[1]))
+            loads(chip, shard).start()
+
+    def merge(chip, shard):
+        await_at(side.at[chip, shard], side_recv.at[chip, shard])
+        loads(chip, shard).wait()
+        add_into(side.at[chip, shard], local.at[chip, shard], rows)
+
+    def first(step):
+        shard = order[step]
+        merge(0, shard)
+        for axis, bit in ((0, 2), (1, 4)):
+            at = pl.ds(axis * half, half)
+            start(send(side.at[0, shard, at], on.at[axis, shard], on_send.at[axis, shard], on_recv.at[axis, shard], close[bit]))
+        merge(1, shard)
+        merge(2, shard)
+
+    def second(step):
+        shard = order[step]
+        for axis, bit in ((0, 2), (1, 4)):
+            other = 2 - axis
+            await_at(on.at[axis, shard], on_recv.at[axis, shard])
+            add_into(side.at[other, shard], on.at[axis, shard], half, axis * half, 0)
+            start(send(side.at[other, shard], near.at[1 - axis, shard], near_send.at[1 - axis, shard], near_recv.at[1 - axis, shard], close[6 - bit]))
+        merge(3, shard)
+
+    def third(step):
+        shard = order[step]
+        for axis in (0, 1):
+            await_at(near.at[axis, shard], near_recv.at[axis, shard])
+            add_into(side.at[3, shard], near.at[axis, shard], rows)
+
+    def fourth(step):
+        shard = order[step]
+        if step < n - 1:
+            for way in (0, 1):
+                ahead = shard > spot if way == 0 else shard < spot
+                distance = jnp.clip(shard - spot if way == 0 else spot - shard, 1, n - 1)
+
+                @pl.when(ahead & sides[1 - way][0])
+                def _(way=way, distance=distance):
+                    slot = jnp.minimum(distance, n - 2)
+                    await_at(chain.at[way, slot], z_recv.at[way, slot])
+                    add_into(side.at[3, shard], chain.at[way, slot], rows)
+
+                start(send(side.at[3, shard], chain.at[way, distance - 1], z_send.at[way, distance - 1], z_recv.at[way, distance - 1], sides[way][1]), ahead)
+        else:
+
+            def body(index, carry):
+                at = pl.ds(pl.multiple_of(index * 16, 16), 16)
+                out[at, :] = side[3, spot, at, :].astype(jnp.float32)
+                return carry
+
+            lax.fori_loop(0, rows // 16, body, 0)
+            for way in (0, 1):
+
+                @pl.when(sides[1 - way][0])
+                def _(way=way):
+                    await_at(chain.at[way, 0], z_recv.at[way, 0])
+                    add_into(out, chain.at[way, 0], rows)
+
+    for step in range(n + 3):
+        for task, delay in ((first, 0), (second, 1), (third, 2), (fourth, 3)):
+            if 0 <= step - delay < n:
+                task(step - delay)
+    for condition, one in sends:
+        if condition is None:
+            one.wait_send()
+        else:
+
+            @pl.when(condition)
+            def _(one=one):
+                one.wait_send()
+
+
+def box_sum(part, later):
+    n = lax.axis_size("tensor")
+    width = part.shape[1]
+    rows = part.shape[0] // (8 * n)
+    sem = pltpu.SemaphoreType.DMA
+    kind = part.dtype
+    anywhere = pl.BlockSpec(memory_space=pl.ANY)
+    return pl.pallas_call(
+        functools.partial(box_sum_kernel, n),
+        out_shape=[
+            jax.ShapeDtypeStruct((rows, width), jnp.float32),
+            jax.ShapeDtypeStruct(later.shape, later.dtype),
+        ],
+        in_specs=[anywhere] * 2,
+        out_specs=[pl.BlockSpec(memory_space=pltpu.VMEM), anywhere],
+        input_output_aliases={1: 1},
+        scratch_shapes=[
+            pltpu.VMEM((4, n, rows, width), kind),
+            pltpu.VMEM((4, n, rows, width), kind),
+            pltpu.VMEM((2, n, rows // 2, width), kind),
+            pltpu.VMEM((2, n, rows, width), kind),
+            pltpu.VMEM((2, n - 1, rows, width), kind),
+            sem((4, n)),
+            sem((4, n)),
+            sem((4, n)),
+            sem((2, n)),
+            sem((2, n)),
+            sem((2, n)),
+            sem((2, n)),
+            sem((2, n - 1)),
+            sem((2, n - 1)),
+        ],
+        compiler_params=pltpu.CompilerParams(
+            collective_id=4, has_side_effects=True, vmem_limit_bytes=VMEM
+        ),
+        cost_estimate=transfer(165),
+        name="box_sum",
+    )(part.reshape(8, n, rows, width), later)
+
+
+def everyone(n):
+    count = lax.axis_size("dp") * n
+    me = lax.axis_index("dp") * n + lax.axis_index("tensor")
+
+    def device(number):
+        return {"dp": number // n, "tensor": number % n}
+
+    return count, me, device
+
+
+def greet_all(count, me, device):
+    barrier = pltpu.get_barrier_semaphore()
+
+    def signal(step, carry):
+        pl.semaphore_signal(barrier, inc=1, device_id=device(lax.rem(me + step, count)), device_id_type=MESH)
+        return carry
+
+    lax.fori_loop(1, count, signal, 0)
+    pl.semaphore_wait(barrier, count - 1)
+
+
+def spread_kernel(n, own, out, send_sem, recv_sem):
+    count, me, device = everyone(n)
+    greet_all(count, me, device)
+    out[me] = own[...]
+
+    def copy(step):
+        return send(own, out.at[me], send_sem.at[step], recv_sem.at[step], device(lax.rem(me + step, count)))
+
+    def go(step, carry):
+        copy(step).start()
+        return carry
+
+    def end(step, carry):
+        copy(step).wait_send()
+        come = lax.rem(me - step + count, count)
+        send(own, out.at[come], send_sem.at[step], recv_sem.at[step], device(come)).wait_recv()
+        return carry
+
+    lax.fori_loop(1, count, go, 0)
+    lax.fori_loop(1, count, end, 0)
+
+
+def spread(own):
+    n = lax.axis_size("tensor")
+    count = lax.axis_size("dp") * n
+    sem = pltpu.SemaphoreType.DMA
+    return pl.pallas_call(
+        functools.partial(spread_kernel, n),
+        out_shape=jax.ShapeDtypeStruct((count,) + own.shape, own.dtype),
+        in_specs=[pl.BlockSpec(memory_space=pltpu.VMEM)],
+        out_specs=pl.BlockSpec(memory_space=pltpu.VMEM),
+        scratch_shapes=[sem((count,)), sem((count,))],
+        compiler_params=pltpu.CompilerParams(
+            collective_id=5, has_side_effects=True, vmem_limit_bytes=VMEM
+        ),
+        cost_estimate=transfer(10),
+        name="spread",
+    )(own)
+
+
+def sum_spread_kernel(n, part, out, held, send_sem, recv_sem):
+    count, me, device = everyone(n)
+    greet_all(count, me, device)
+    out[...] = part[me]
+
+    def copy(step):
+        to = lax.rem(me + step, count)
+        return send(part.at[to], held.at[me], send_sem.at[step], recv_sem.at[step], device(to))
+
+    def go(step, carry):
+        copy(step).start()
+        return carry
+
+    def end(step, carry):
+        come = lax.rem(me - step + count, count)
+        send(part.at[0], held.at[come], send_sem.at[step], recv_sem.at[step], device(come)).wait_recv()
+        out[...] += held[come]
+        copy(step).wait_send()
+        return carry
+
+    lax.fori_loop(1, count, go, 0)
+    lax.fori_loop(1, count, end, 0)
+
+
+def sum_spread(part):
+    n = lax.axis_size("tensor")
+    count = lax.axis_size("dp") * n
+    sem = pltpu.SemaphoreType.DMA
+    return pl.pallas_call(
+        functools.partial(sum_spread_kernel, n),
+        out_shape=jax.ShapeDtypeStruct(part.shape[1:], part.dtype),
+        in_specs=[pl.BlockSpec(memory_space=pltpu.VMEM)],
+        out_specs=pl.BlockSpec(memory_space=pltpu.VMEM),
+        scratch_shapes=[pltpu.VMEM(part.shape, part.dtype), sem((count,)), sem((count,))],
+        compiler_params=pltpu.CompilerParams(
+            collective_id=6, has_side_effects=True, vmem_limit_bytes=VMEM
+        ),
+        cost_estimate=transfer(20),
+        name="sum_spread",
+    )(part)
+
+
 TB = 256
 GR = 16
 TILE = 256
 SLOTS = 512
 EXTRA = 2 * E
-VMEM = 60 * 1024 * 1024
-
-
 def ceil_to(value, unit):
     return (value + unit - 1) // unit * unit
 
@@ -532,6 +1128,63 @@
     )
 
 
+def gather_all(own):
+    if lax.axis_size("dp") == 8:
+        return box_gather(own)
+    return lax.all_gather(
+        lax.all_gather(own, "tensor", axis=0, tiled=True), "dp", axis=0, tiled=True
+    )
+
+
+def gather_slowly(own):
+    if lax.axis_size("dp") == 8:
+        return lax.all_gather(own, ("dp", "tensor"), axis=0, tiled=True)
+    return gather_all(own)
+
+
+def sum_all(part, later):
+    if lax.axis_size("dp") == 8:
+        return box_sum(part, later)
+    return chain_sum(lax.psum_scatter(part, "dp", scatter_dimension=0, tiled=True), later, 9)
+
+
+def fill(value, rows, columns):
+    return jnp.pad(value, ((0, rows - value.shape[0]), (0, columns - value.shape[1])))
+
+
+def share_small(router, prenorm, postnorm, querynorm, keynorm, routes):
+    n = lax.axis_size("tensor")
+    rank = lax.axis_index("tensor")
+    rows = router.shape[0]
+    head = ceil_to(max(rows, querynorm.shape[0]), 16)
+    heads = querynorm.shape[1]
+    block = jnp.concatenate(
+        [
+            fill(router, head, E),
+            fill(prenorm[:, None], head, 1),
+            fill(postnorm[:, None], head, 1),
+            fill(querynorm, head, heads),
+            fill(keynorm, head, heads),
+        ],
+        1,
+    )
+    part = routes.shape[0] // n
+    own = lax.dynamic_slice_in_dim(routes, rank * part, part, 0)
+    own = own.astype(jnp.bfloat16).reshape(-1, 128)
+    tail = ceil_to(own.shape[0], 16)
+    everything = spread(jnp.concatenate([fill(block, head, 128), fill(own, tail, 128)], 0))
+    mine = everything.reshape(-1, n, head + tail, 128)[:, rank]
+    at = E + 2
+    return (
+        everything[:, :rows, :E].reshape(-1, E),
+        everything[:, :rows, E].reshape(-1).astype(jnp.float32),
+        everything[:, :rows, E + 1].reshape(-1).astype(jnp.float32),
+        mine[:, : querynorm.shape[0], at : at + heads].reshape(-1, heads),
+        mine[:, : querynorm.shape[0], at + heads : at + 2 * heads].reshape(-1, heads),
+        everything[:, head : head + own.shape[0]].reshape(-1, TOP).astype(jnp.int32),
+    )
+
+
 def body(
     hidden_in,
     out_grad,
@@ -560,31 +1213,27 @@
     block = min(seq_len, 1024)
     scale = HD ** (-0.5)
     cosine, sine = rope_tables(seq_len, HD)
-    router_full, pre_gain, post_gain = (
-        lax.all_gather(router, ("dp", "tensor"), axis=0, tiled=True),
-        lax.all_gather(prenorm, ("dp", "tensor"), axis=0, tiled=True),
-        lax.all_gather(postnorm, ("dp", "tensor"), axis=0, tiled=True),
-    )
-    pre_gain = pre_gain.astype(jnp.float32)
-    post_gain = post_gain.astype(jnp.float32)
-    w_query, w_key, w_value, w_output, gain_query, gain_key = (
-        lax.all_gather(query_proj, "dp", axis=0, tiled=True),
-        lax.all_gather(key_proj, "dp", axis=0, tiled=True),
-        lax.all_gather(value_proj, "dp", axis=0, tiled=True),
-        lax.all_gather(output_proj, "dp", axis=0, tiled=True),
-        lax.all_gather(querynorm, "dp", axis=0, tiled=True),
-        lax.all_gather(keynorm, "dp", axis=0, tiled=True),
-    )
+    router_full, pre_gain, post_gain, gain_query, gain_key, all_routes = share_small(
+        router, prenorm, postnorm, querynorm, keynorm, routes
+    )
+    weights = lax.all_gather(
+        jnp.concatenate([query_proj, key_proj, value_proj, output_proj], 1),
+        "dp",
+        axis=0,
+        tiled=True,
+    )
+    w_query, w_key, w_value, w_output = jnp.split(weights, 4, 1)
     heads = w_query.shape[1] // HD
     query_scale = gain_query.astype(jnp.float32).T.reshape(-1)
     key_scale = gain_key.astype(jnp.float32).T.reshape(-1)
     inv_pre = lax.rsqrt(jnp.mean(residual * residual, -1, keepdims=True) + epsilon)
-    normed = (residual * inv_pre * pre_gain).astype(jnp.bfloat16)
-    (group_normed,) = gather_tokens((normed,))
+    group_hidden, later = chain_gather(hidden_in[0], upstream, 1)
+    group_hidden = group_hidden.astype(jnp.float32)
+    group_inv = lax.rsqrt(jnp.mean(group_hidden * group_hidden, -1, keepdims=True) + epsilon)
+    group_normed = (group_hidden * group_inv * pre_gain).astype(jnp.bfloat16)
     plan = Plan(mesh_dp * seq_len, seq_len, gate_proj.shape[0])
     base = (lax.axis_index("dp") * plan.local).astype(jnp.int32)
-    all_routes = lax.all_gather(routes, "dp", axis=0, tiled=True)
-    all_grad = lax.all_gather(upstream, ("dp", "tensor"), axis=0, tiled=True)
+    all_grad = gather_slowly(later)
     route = routing(plan, all_routes, base)
     query = jnp.dot(group_normed, w_query, preferred_element_type=jnp.float32)
     keys = jnp.dot(group_normed, w_key, preferred_element_type=jnp.float32)
@@ -606,11 +1255,11 @@
     attn_term = lax.dot_general(
         mixed_flat, w_output, (((1,), (1,)), ((), ())), preferred_element_type=jnp.float32
     )
-    attn_local = sum_tokens(attn_term)
+    attn_local, later = chain_sum(attn_term.astype(jnp.bfloat16), later, 7)
     middle = residual + attn_local
     inv_post = lax.rsqrt(jnp.mean(middle * middle, -1, keepdims=True) + epsilon)
     post_normed = (middle * inv_post * post_gain).astype(jnp.bfloat16)
-    all_post = lax.all_gather(post_normed, ("dp", "tensor"), axis=0, tiled=True)
+    all_post = gather_all(post_normed)
     rows = dispatch(plan, route, all_post, all_grad, router_full)
     results, gate_weight_grad, up_weight_grad, down_weight_grad = experts(
         plan, route, base, rows[0], gate_proj, up_proj, down_proj
@@ -618,15 +1267,15 @@
     moe_term, grad_term, router_part = combine(
         plan, route, results, rows[1], all_post, router_full
     )
-    moe_local = sum_all(moe_term)
-    grad_post = sum_all(grad_term)
+    grad_post, moe_term = sum_all(grad_term, moe_term)
+    moe_term = lax.psum_scatter(moe_term, "dp", scatter_dimension=0, tiled=True)
+    moe_local = lax.psum_scatter(moe_term, "tensor", scatter_dimension=0, tiled=True)
     router_part = router_part.T
-    layer_out = (middle + moe_local).astype(jnp.bfloat16)[None]
     post_gain_part = jnp.sum(grad_post * middle * inv_post, 0)
     grad_middle = upstream.astype(jnp.float32) + norm_back(
         grad_post, middle, inv_post, post_gain, D
     )
-    (group_change,) = gather_tokens((grad_middle.astype(jnp.bfloat16),))
+    group_change, _ = chain_gather(grad_middle.astype(jnp.bfloat16), later, 2)
     grad_mixed = jnp.dot(group_change, w_output, preferred_element_type=jnp.float32).astype(
         jnp.bfloat16
     )
@@ -682,48 +1331,57 @@
     normed_term = normed_term + lax.dot_general(
         grad_value, w_value, (((1,), (1,)), ((), ())), preferred_element_type=jnp.float32
     )
-    grad_normed = sum_tokens(normed_term)
+    grad_normed, middle = chain_sum(normed_term.astype(jnp.bfloat16), middle, 8)
+    layer_out = (middle + moe_local.astype(jnp.float32)).astype(jnp.bfloat16)[None]
     pre_gain_part = jnp.sum(grad_normed * residual * inv_pre, 0)
     input_grad = (grad_middle + norm_back(grad_normed, residual, inv_pre, pre_gain, D)).astype(
         jnp.bfloat16
     )[None]
-    attn_sums = (
-        lax.psum_scatter(
-            query_part.astype(jnp.bfloat16), "dp", scatter_dimension=0, tiled=True
-        ).astype(jnp.float32),
-        lax.psum_scatter(
-            key_part.astype(jnp.bfloat16), "dp", scatter_dimension=0, tiled=True
-        ).astype(jnp.float32),
-        lax.psum_scatter(
-            value_part.astype(jnp.bfloat16), "dp", scatter_dimension=0, tiled=True
-        ).astype(jnp.float32),
-        lax.psum_scatter(
-            output_part.astype(jnp.bfloat16), "dp", scatter_dimension=0, tiled=True
-        ).astype(jnp.float32),
-        lax.psum_scatter(
-            query_gain_part.astype(jnp.bfloat16), "dp", scatter_dimension=0, tiled=True
-        ).astype(jnp.float32),
-        lax.psum_scatter(
-            key_gain_part.astype(jnp.bfloat16), "dp", scatter_dimension=0, tiled=True
-        ).astype(jnp.float32),
-    )
-    small_sums = (
-        lax.psum_scatter(router_part, ("dp", "tensor"), scatter_dimension=0, tiled=True),
-        lax.psum_scatter(pre_gain_part, ("dp", "tensor"), scatter_dimension=0, tiled=True),
-        lax.psum_scatter(post_gain_part, ("dp", "tensor"), scatter_dimension=0, tiled=True),
-    )
+    own_rows = D // mesh_dp
+    gains = jnp.concatenate([query_gain_part, key_gain_part], 1).astype(jnp.bfloat16)
+    gains = jnp.pad(
+        gains.reshape(mesh_dp, -1, 2 * heads),
+        ((0, 0), (0, own_rows - HD // mesh_dp), (0, 128 - 2 * heads)),
+    )
+    attn_sums = lax.psum_scatter(
+        jnp.concatenate(
+            [
+                part.astype(jnp.bfloat16)
+                for part in (query_part, key_part, value_part, output_part)
+            ]
+            + [gains.reshape(D, 128)],
+            1,
+        ),
+        "dp",
+        scatter_dimension=0,
+        tiled=True,
+    ).astype(jnp.float32)
+    query_grad, key_grad, value_grad, output_grad, gain_grads = jnp.split(
+        attn_sums, [heads * HD * count for count in (1, 2, 3, 4)], 1
+    )
+    gain_grads = gain_grads[: HD // mesh_dp]
+    small = jnp.concatenate(
+        [
+            router_part,
+            pre_gain_part[:, None],
+            post_gain_part[:, None],
+            jnp.zeros((D, 128 - E - 2), jnp.float32),
+        ],
+        1,
+    )
+    small = sum_spread(small.reshape(-1, router.shape[0], 128))
     return (
         layer_out,
         input_grad,
-        small_sums[1],
-        attn_sums[4],
-        attn_sums[5],
-        attn_sums[0],
-        attn_sums[1],
-        attn_sums[2],
-        attn_sums[3],
-        small_sums[2],
-        small_sums[0],
+        small[:, E],
+        gain_grads[:, :heads],
+        gain_grads[:, heads : 2 * heads],
+        query_grad,
+        key_grad,
+        value_grad,
+        output_grad,
+        small[:, E + 1],
+        small[:, :E],
         gate_weight_grad,
         up_weight_grad,
         down_weight_grad,

time: 2310 us -> 1560 us (0.68)
  waiting for transfers between devices: 1380 us -> 102 us
  Pallas kernels: 463 us -> 1180 us
  blocking collectives: 226 us -> 22.8 us
    reduce_scatter x10 -> x3, waiting for transfers between devices: 759 us -> 34.2 us  [the longest x1 33.9 us: body(): moe_term = lax.psum_scatter(moe_term, 'dp', scatter_dimension=0, tiled=True)]
    pallas_call x0 -> x8, Pallas kernels: none -> 699 us  [the longest x1 168 us: box_sum(): pl.pallas_call(functools.partial(box_sum_kernel, n), out_shape=[jax.Shape...]
    all_gather x8 -> x2, waiting for transfers between devices: 414 us -> 67.7 us  [the longest x1 67.7 us: gather_slowly(): return lax.all_gather(own, ('dp', 'tensor'), axis=0, tiled=True)]
    unnamed x24 -> x5, waiting for transfers between devices: 204 us -> 0.08 us
    all_gather x4 -> x0, blocking collectives: 121 us -> none  [the longest x1 93.6 us: body(): lax.all_gather(router, ('dp', 'tensor'), axis=0, tiled=True)]
    unnamed x2 -> x0, blocking collectives: 85.2 us -> none
  transfers between devices with their start and end apart: 21 -> 5, of which waited for: 19 -> 3; matrix products, arithmetic and copies ran while one was open for 8% -> 13% of each run, Pallas kernels for 0% -> 20%
where the time goes in v2:
time: 1560 us; the launch traced here: 1550 us
  Pallas kernels  1180 us (76%)
  matrix products  106 us (7%)
  waiting for transfers between devices  102 us (7%)
  other arithmetic  77.8 us (5%)
  local copies, waits for them, and re-layouts  45.8 us (3%)
  blocking collectives  22.8 us (1%)
  between operations  16.4 us (1%)
    pallas_call x1, Pallas kernels, experts(): pl.pallas_call(expert_kernel, grid_spec=pltpu.PrefetchScalarGridSpec(num_...  185 us
    pallas_call x1, Pallas kernels, box_sum(): pl.pallas_call(functools.partial(box_sum_kernel, n), out_shape=[jax.Shape...  168 us
    pallas_call x1, Pallas kernels, dispatch(): pl.pallas_call(dispatch_kernel, grid_spec=pltpu.PrefetchScalarGridSpec(nu...  157 us
    pallas_call x2, Pallas kernels, chain_sum(): pl.pallas_call(functools.partial(chain_sum_kernel, n, pieces), out_shape=...  149 us
    pallas_call x2, Pallas kernels, chain_gather(): pl.pallas_call(functools.partial(chain_gather_kernel, n, pieces), out_sha...  148 us
    pallas_call x1, Pallas kernels, box_gather(): pl.pallas_call(functools.partial(box_gather_kernel, n), out_shape=jax.Sha...  144 us
    pallas_call x1, Pallas kernels, combine(): pl.pallas_call(combine_kernel, grid_spec=pltpu.PrefetchScalarGridSpec(num...  135 us
    all_gather x1, waiting for transfers between devices, gather_slowly(): return lax.all_gather(own, ('dp', 'tensor'), axis=0, tiled=True)  67.7 us
  transfers between devices with their start and end apart: 5, of which 3 were waited for; matrix products, arithmetic and copies ran while one was open for 13% of the time, Pallas kernels for 20%

profile of v2, /device:TPU:0, one launch (start us, length us, event | category | flops | bytes accessed | tf_op | source)
XLA Modules:
  0.0 1547.0 jit_solution(10052249426054807959)
XLA Ops:
  10.7 73.3 %chain_gather.2 = (bf16[4,256,2048]{2,1,0:T(8,128)(2,1)}, bf16[256,2048]{1,0:T(8,128)(2,1)}) custom-call(bf16[256,2048]{1,0:T(8,128)(2,1)} %bitcast.228, bf16[256,2048]{1,0:T(8,128)(2,1)} %copy.227._later), custom_call_target="tpu_custom_call", output_to_operand_aliasing={{1}: (1, {})} | custom-call | bytes 195000000 | tf_op jit(solution)/shard_map/chain_gather/pallas_call | solution.py:218
  86.2 34.4 %spread.1 = bf16[32,80,128]{2,1,0:T(8,128)(2,1)} custom-call(bf16[80,128]{1,0:T(8,128)(2,1)} %fusion.77.own), custom_call_target="tpu_custom_call" | custom-call | bytes 30000000 | tf_op jit(solution)/shard_map/spread/pallas_call | solution.py:671
  152.2 6.7 multiply_reduce_fusion.6
  163.1 10.9 all-reduce.5
  185.1 12.3 fusion.104
  197.4 8.1 fusion
  205.6 7.8 fusion.52
  220.4 67.7 %all-gather.5.cloned.1.call-done.grad = bf16[8192,2048]{1,0:T(8,128)(2,1)} async-done(((bf16[256,2048]{1,0:T(8,128)(2,1)}), bf16[8192,2048]{1,0:T(8,128)(2,1)}) %all-gather.5.cloned.1.call-update) | async-done | bytes 33554448 | tf_op jit(solution)/shard_map/all_gather | solution.py:1141
  288.1 72.1 %chain_sum.2 = (f32[256,2048]{1,0:T(8,128)}, bf16[256,2048]{1,0:T(8,128)(2,1)}) custom-call(bf16[4,256,2048]{2,1,0:T(8,128)(2,1)} %bitcast.233, bf16[256,2048]{1,0:T(8,128)(2,1)} %get-tuple-element.84._later), custom_call_target="tpu_custom_call", output_to_operand_aliasing={{1}: (1, {})} | custom-call | bytes 195000000 | tf_op jit(solution)/shard_map/chain_sum/pallas_call | solution.py:335
  365.4 143.5 %box_gather.1 = bf16[8,4,256,2048]{3,2,1,0:T(8,128)(2,1)} custom-call(bf16[256,2048]{1,0:T(8,128)(2,1)} %multiply_convert_fusion.2.own), custom_call_target="tpu_custom_call" | custom-call | bytes 420000000 | tf_op jit(solution)/shard_map/box_gather/pallas_call | solution.py:447
  508.9 156.9 %dispatch.1 = (bf16[24320,4224]{1,0:T(8,128)(2,1)}, bf16[8192,128]{1,0:T(8,128)(2,1)}) custom-call(s32[1]{0:T(128)} %bitcast.33.used, s32[95]{0:T(128)} %copy-done.71, s32[95]{0:T(128)} %fusion.90.part, bf16[8192,2048]{1,0:T(8,128)(2,1)} %bitcast.220, bf16[8192,2048]{1,0:T(8,128)(2,1)} %all-gather.5.cloned.1.call-done.grad, bf16[2048,64]{1,0:T(8,128)(2,1)} %bitcast.241, ...), custom_call_target="tpu_custom_call" | custom-call | flops 52596572160 | bytes 410910720 | tf_op jit(solution)/shard_map/dispatch/pallas_call | solution.py:872
  665.9 184.6 %experts.1 = (bf16[16384,4224]{1,0:T(8,128)(2,1)}, f32[8,2048,256]{2,1,0:T(8,128)}, f32[8,2048,256]{2,1,0:T(8,128)}, f32[8,2048,256]{2,1,0:T(8,128)}) custom-call(s32[1024]{0:T(1024)} %bitcast.267, s32[8]{0:T(128)} %get-tuple-element.266.tiles, s32[8]{0:T(128)} %get-tuple-element.265.filled, s32[1]{0:T(128)} %bitcast.32.base, ...), custom_call_target="tpu_custom_call" | custom-call | flops 96636764160 | bytes 173015040 | tf_op jit(solution)/shard_map/experts/pallas_call | solution.py:986
  850.5 135.1 %combine.1 = (bf16[8192,2048]{1,0:T(8,128)(2,1)}, bf16[8192,2048]{1,0:T(8,128)(2,1)}, f32[64,2048]{1,0:T(8,128)}) custom-call(s32[1]{0:T(128)} %bitcast.25.joined, s32[63]{0:T(128)} %copy-done.60, s32[63]{0:T(128)} %copy-done.61, s32[63]{0:T(128)} %compare_convert_fusion.last, s32[2016]{0:T(1024)} %reshape.656.target, ...), custom_call_target="tpu_custom_call" | custom-call | flops 69759664128 | bytes 138412032 | tf_op jit(solution)/shard_map/combine/pallas_call | solution.py:1086
  985.7 168.3 %box_sum.1 = (f32[256,2048]{1,0:T(8,128)}, bf16[8192,2048]{1,0:T(8,128)(2,1)}) custom-call(bf16[8,4,256,2048]{3,2,1,0:T(8,128)(2,1)} %bitcast.222, bf16[8192,2048]{1,0:T(8,128)(2,1)} %get-tuple-element.90._later), custom_call_target="tpu_custom_call", output_to_operand_aliasing={{1}: (1, {})} | custom-call | bytes 495000000 | tf_op jit(solution)/shard_map/box_sum/pallas_call | solution.py:591
  1164.4 74.8 %chain_gather.3 = (bf16[4,256,2048]{2,1,0:T(8,128)(2,1)}, bf16[256,2048]{1,0:T(8,128)(2,1)}) custom-call(bf16[256,2048]{1,0:T(8,128)(2,1)} %get-tuple-element.212.own, bf16[256,2048]{1,0:T(8,128)(2,1)} %get-tuple-element.92._later), custom_call_target="tpu_custom_call", output_to_operand_aliasing={{1}: (1, {})} | custom-call | bytes 195000000 | tf_op jit(solution)/shard_map/chain_gather/pallas_call | solution.py:218
  1244.5 14.8 multiply_reduce_fusion
  1262.2 8.3 multiply_convert_fusion
  1274.1 6.6 bitcast_multiply_fusion.4
  1289.2 11.9 all-reduce.4
  1317.9 6.3 fusion.10
  1329.0 33.9 %reduce-scatter.4.cloned.1.call-done = bf16[1024,2048]{1,0:T(8,128)(2,1)} async-done(((bf16[8192,2048]{1,0:T(8,128)(2,1)}), bf16[1024,2048]{1,0:T(8,128)(2,1)}) %reduce-scatter.4.cloned.1.call-update) | async-done | bytes 4194320 | tf_op jit(solution)/shard_map/reduce_scatter | solution.py:1271
  1372.3 6.4 add_convert_fusion
  1378.7 77.1 %chain_sum.3 = (f32[256,2048]{1,0:T(8,128)}, f32[256,2048]{1,0:T(8,128)}) custom-call(bf16[4,256,2048]{2,1,0:T(8,128)(2,1)} %bitcast.229, f32[256,2048]{1,0:T(8,128)} %copy-done), custom_call_target="tpu_custom_call", output_to_operand_aliasing={{1}: (1, {})} | custom-call | bytes 195000000 | tf_op jit(solution)/shard_map/chain_sum/pallas_call | solution.py:335
  1466.9 55.3 %sum_spread.1 = f32[64,128]{1,0:T(8,128)} custom-call(f32[32,64,128]{2,1,0:T(8,128)} %maximum_maximum_fusion.part), custom_call_target="tpu_custom_call" | custom-call | bytes 60000000 | tf_op jit(solution)/shard_map/sum_spread/pallas_call | solution.py:713
  (311 shorter events, 153.3 us)
Async XLA Ops:
  7.2 145.0 %all-gather.3.cloned.1.call-start = ((), (), s32[]{:S(2)}) async-start(), calls=%async_computation.3 | async-start | bytes 9437184 | tf_op jit(solution)/shard_map/all_gather | solution.py:1219
  9.6 278.5 %all-gather.5.cloned.1.call-start = ((), (), s32[]{:S(2)}) async-start(), calls=%async_computation.4 | async-start | bytes 34603008 | tf_op jit(solution)/shard_map/all_gather | solution.py:1141
  10.7 73.4 %copy-start.66 = (bf16[64]{0:T(256)(128)(2,1)S(1)}, bf16[64]{0:T(256)(128)(2,1)}, u32[]{:S(2)}) copy-start(bf16[64]{0:T(256)(128)(2,1)} %param.20) | copy-start | bytes 388
  10.7 73.5 %copy-start.67 = (bf16[64]{0:T(256)(128)(2,1)S(1)}, bf16[64]{0:T(256)(128)(2,1)}, u32[]{:S(2)}) copy-start(bf16[64]{0:T(256)(128)(2,1)} %param.27) | copy-start | bytes 388
  10.7 73.6 %copy-start.64 = (bf16[16,4]{0,1:T(4,128)(2,1)S(1)}, bf16[16,4]{0,1:T(4,128)(2,1)}, u32[]{:S(2)}) copy-start(bf16[16,4]{0,1:T(4,128)(2,1)} %param.21) | copy-start | bytes 388
  10.7 73.7 %copy-start.65 = (bf16[16,4]{0,1:T(4,128)(2,1)S(1)}, bf16[16,4]{0,1:T(4,128)(2,1)}, u32[]{:S(2)}) copy-start(bf16[16,4]{0,1:T(4,128)(2,1)} %param.22) | copy-start | bytes 388
  10.7 74.8 %copy-start.55 = (bf16[64,64]{1,0:T(8,128)(2,1)S(1)}, bf16[64,64]{1,0:T(8,128)(2,1)}, u32[]{:S(2)}) copy-start(bf16[64,64]{1,0:T(8,128)(2,1)} %param.28) | copy-start | bytes 24580
  84.0 1278.9 %reduce-scatter.4.cloned.1.call-start = ((), (), s32[]{:S(2)}) async-start(), calls=%async_computation.5 | async-start | bytes 37748736 | tf_op jit(solution)/shard_map/reduce_scatter | solution.py:1271
  131.2 18.0 %copy-start.36 = (f32[2048]{0:T(1024)}, f32[2048]{0:T(1024)S(1)}, u32[]{:S(2)}) copy-start(f32[2048]{0:T(1024)S(1)} %reshape.673) | copy-start | bytes 24580
  135.1 39.5 %copy-start.51 = (f32[128,4]{0,1:T(4,128)}, f32[128,4]{0,1:T(4,128)S(1)}, u32[]{:S(2)}) copy-start(f32[128,4]{0,1:T(4,128)S(1)} %copy.186) | copy-start | bytes 6148
  135.2 41.5 %copy-start.49 = (f32[128,4]{0,1:T(4,128)}, f32[128,4]{0,1:T(4,128)S(1)}, u32[]{:S(2)}) copy-start(f32[128,4]{0,1:T(4,128)S(1)} %copy.187) | copy-start | bytes 6148
  140.2 223.3 %copy-start.40 = (f32[2048]{0:T(1024)}, f32[2048]{0:T(1024)S(1)}, u32[]{:S(2)}) copy-start(f32[2048]{0:T(1024)S(1)} %reshape.677) | copy-start | bytes 24580
  185.1 20.5 %copy-start.23 = (bf16[1024,512]{0,1:T(8,128)(2,1)}, bf16[1024,512]{0,1:T(8,128)(2,1)S(1)}, u32[]{:S(2)}) copy-start(bf16[1024,512]{0,1:T(8,128)(2,1)S(1)} %fusion.53) | copy-start | bytes 3145732
  288.1 72.1 %copy-start.8 = (bf16[1,256,2048]{2,1,0:T(8,128)(2,1)S(1)}, bf16[1,256,2048]{2,1,0:T(8,128)(2,1)}, u32[]{:S(2)}) copy-start(bf16[1,256,2048]{2,1,0:T(8,128)(2,1)} %param.16) | copy-start | bytes 3145732
  1154.0 372.9 %reduce-scatter.8.cloned.1.call-start = ((), (), s32[]{:S(2)}) async-start(), calls=%async_computation.7 | async-start | bytes 10027008 | tf_op jit(solution)/shard_map/reduce_scatter | solution.py:1346
  1244.4 16.4 %slice-start.2 = ((s8[16777216]{0:T(1024)(128)(4,1)}), s8[4194304]{0:T(1024)(128)(4,1)S(1)}, s32[]{:S(2)}) async-start(s8[16777216]{0:T(1024)(128)(4,1)} %bitcast.216), calls=%async_computation.10 | async-start | bytes 8388608
  1244.4 17.8 %slice-start.3 = ((s8[16777216]{0:T(1024)(128)(4,1)}), s8[4194304]{0:T(1024)(128)(4,1)S(1)}, s32[]{:S(2)}) async-start(s8[16777216]{0:T(1024)(128)(4,1)} %bitcast.216), calls=%async_computation.11 | async-start | bytes 8388608
  1285.1 16.1 %copy-start.57 = (f32[1024,1]{0,1:T(1,128)S(1)}, f32[1024,1]{0,1:T(1,128)}, u32[]{:S(2)}) copy-start(f32[1024,1]{0,1:T(1,128)} %get-tuple-element.284) | copy-start | bytes 12292
  1285.1 18.9 %copy-start.56 = (f32[1024,1]{0,1:T(1,128)S(1)}, f32[1024,1]{0,1:T(1,128)}, u32[]{:S(2)}) copy-start(f32[1024,1]{0,1:T(1,128)} %get-tuple-element.208) | copy-start | bytes 12292
  1328.8 208.4 %reduce-scatter.6.cloned.1.call-start = ((), (), s32[]{:S(2)}) async-start(), calls=%async_computation.6 | async-start | bytes 5242880 | tf_op jit(solution)/shard_map/reduce_scatter | solution.py:1272
  1378.7 77.2 %copy-start.48 = (f32[2048]{0:T(1024)S(1)}, f32[2048]{0:T(1024)}, u32[]{:S(2)}) copy-start(f32[2048]{0:T(1024)} %get-tuple-element.189) | copy-start | bytes 24580
  1378.7 79.0 %copy-start.62 = (f32[256]{0:T(256)S(1)}, f32[256]{0:T(256)}, u32[]{:S(2)}) copy-start(f32[256]{0:T(256)} %get-tuple-element.241) | copy-start | bytes 3076
  1378.7 79.0 %copy-start.9 = (bf16[1,256,2048]{2,1,0:T(8,128)(2,1)S(1)}, bf16[1,256,2048]{2,1,0:T(8,128)(2,1)}, u32[]{:S(2)}) copy-start(bf16[1,256,2048]{2,1,0:T(8,128)(2,1)} %param.16) | copy-start | bytes 3145732
  1463.2 60.5 %copy-start.15 = (f32[256,2048]{1,0:T(8,128)S(1)}, f32[256,2048]{1,0:T(8,128)}, u32[]{:S(2)}) copy-start(f32[256,2048]{1,0:T(8,128)} %get-tuple-element.96) | copy-start | bytes 6291460
  (61 other events, 275.0 us)
Sparse Core Ops, SparseCore 0:
  10.5 57.0 all-gather.2
  84.1 203.9 all-gather.4
  1154.1 208.7 reduce-scatter.3
  1366.8 73.7 reduce-scatter.7
  1442.9 94.2 reduce-scatter.5
